TPU v7x, 256 devices: a whole 4x4x8 slice. The times are simulated.
256 devices in a mesh: ctx: 64 (over z, x, y_lo), head: 4 (over y_hi, core).
Axes of the slice: x: 4, y: 4 (y_hi: 2, y_lo: 2; y = y_hi * 2 + y_lo), z: 8, core: 2. Of those that a mesh axis runs over, the one named last changes fastest.
Arguments:
- queries: bfloat16 [24576, 1024], P('ctx', 'head'), may hold values from -80 to 80
- key_rows: bfloat16 [24576, 128], P(('ctx', 'head')), may hold values from -9 to 9
- value_rows: bfloat16 [24576, 128], P(('ctx', 'head')), may hold values from -6 to 6
- doc_lengths: int32 [64], replicated, may hold values from 1 to 6144, 24576 in all
Outputs:
- attended: bfloat16 [24576, 1024], P('ctx', 'head')
Inputs may be any that keep to these rules, and one draw needn't show every extreme that they name: `doc_lengths`: lengths of documents in order; they fill all 24576 positions and the longest has exactly 6144.
All inputs are finite; a program needn't handle non-finite values.
Results may differ from a plain program's by a relative error of at most 0.0045.
Values may be sent and summed in bfloat16 or wider, within the bound.
No kernel may reach another device: no remote copies, remote signals or barrier semaphores. Data moves between devices by JAX's collectives and lax.ppermute only.
A program may use at most 64 MiB of HBM per device.

v0:
```python
import jax
import jax.numpy as jnp
from jax import lax
from jax.sharding import PartitionSpec as P

NEG = -1e30


def passed_along(shard, axis, by):
    devices = lax.axis_size(axis)
    pairs = [(i, i + by) for i in range(devices) if 0 <= i + by < devices]
    return lax.ppermute(shard, axis, pairs)


def doc_index(positions, doc_ends):
    return jnp.sum((positions[:, None] >= doc_ends[None, :]).astype(jnp.int32), axis=1)


def block_terms(query_heads, q_pos, q_doc, kv_block, key_start, doc_ends):
    head_dim = query_heads.shape[2]
    key_count = kv_block.shape[0]
    key_block = kv_block[:, :head_dim]
    value_block = kv_block[:, head_dim:]
    k_pos = key_start + jnp.arange(key_count, dtype=jnp.int32)
    k_doc = doc_index(k_pos, doc_ends)
    allowed = (
        (k_pos[None, :] <= q_pos[:, None])
        & (k_doc[None, :] == q_doc[:, None])
        & (k_pos[None, :] >= 0)
    )
    scores = jnp.einsum(
        "qhd,kd->qhk", query_heads, key_block, preferred_element_type=jnp.float32
    ) * head_dim ** (-0.5)
    scores = jnp.where(allowed[:, None, :], scores, NEG)
    block_max = jnp.max(scores, axis=2)
    weights = jnp.where(allowed[:, None, :], jnp.exp(scores - block_max[:, :, None]), 0.0).astype(
        jnp.bfloat16
    )
    block_sum = jnp.sum(weights.astype(jnp.float32), axis=2)
    partial_value = jnp.einsum(
        "qhk,kd->qhd", weights, value_block, preferred_element_type=jnp.float32
    )
    return (block_max, block_sum, partial_value)


def merge_terms(merged, terms):
    run_max, run_sum, run_out = merged
    block_max, block_sum, partial_value = terms
    newest = jnp.maximum(run_max, block_max)
    old_scale = jnp.exp(run_max - newest)
    new_scale = jnp.exp(block_max - newest)
    return (
        newest,
        run_sum * old_scale + block_sum * new_scale,
        run_out * old_scale[:, :, None] + partial_value * new_scale[:, :, None],
    )


def absorb_block(merged, query_heads, q_pos, q_doc, kv_block, key_start, doc_ends):
    return merge_terms(
        merged, block_terms(query_heads, q_pos, q_doc, kv_block, key_start, doc_ends)
    )


def on_device(queries, key_rows, value_rows, doc_lengths):
    doc_ends = jnp.cumsum(doc_lengths)
    row_count = queries.shape[0]
    head_dim = key_rows.shape[1]
    heads_here = queries.shape[1] // head_dim
    query_heads = queries.reshape(row_count, heads_here, head_dim)
    ctx_index = lax.axis_index("ctx")
    cycle_size = lax.axis_size("ctx")
    first_row = ctx_index * row_count
    q_pos = first_row + jnp.arange(row_count, dtype=jnp.int32)
    q_doc = doc_index(q_pos, doc_ends)
    kv_parts = jnp.concatenate([key_rows, value_rows], axis=1)
    kv_own = lax.all_gather(kv_parts, "head", axis=0, tiled=True)
    merged = (
        jnp.full((row_count, heads_here), NEG, jnp.float32),
        jnp.zeros((row_count, heads_here), jnp.float32),
        jnp.zeros((row_count, heads_here, head_dim), jnp.float32),
    )

    def absorb(merged, kv_block, key_start):
        return absorb_block(merged, query_heads, q_pos, q_doc, kv_block, key_start, doc_ends)

    merged = absorb(merged, kv_own, first_row)

    def cycle_step(step_index, carry):
        kv_block, merged = carry
        kv_block = passed_along(kv_block, "ctx", 1)
        return (kv_block, absorb(merged, kv_block, (ctx_index - step_index) * row_count))

    _, merged = lax.fori_loop(1, cycle_size, cycle_step, (kv_own, merged))
    run_max, run_sum, run_out = merged
    result = run_out / run_sum[:, :, None]
    return result.reshape(row_count, heads_here * head_dim).astype(jnp.bfloat16)


def solution(mesh):
    return jax.shard_map(
        on_device,
        mesh=mesh,
        in_specs=(P("ctx", "head"), P(("ctx", "head"), None), P(("ctx", "head"), None), P()),
        out_specs=P("ctx", "head"),
        check_vma=False,
    )
```

profile of v0, /device:TPU:144, one launch (start us, length us, event | category | flops | bytes accessed | tf_op | source)
XLA Modules:
  0.0 863.3 jit_solution(14589957552184414147)
XLA Ops:
  11.6 850.8 %while.20 = (s32[]{:T(128)}, bf16[384,256]{1,0:T(8,128)(2,1)S(1)}, f32[384,2]{0,1:T(2,128)S(1)}, f32[384,2]{0,1:T(2,128)S(1)}, f32[384,2,128]{2,0,1:T(8,128)S(1)...) while((s32[]{:T(128)}, bf16[384,256]{1,0:T(8,128)(2,1)S(1)}, ...), condition=%wide.region_8.9_spmd.clone, body=%wide.region_4.0_spmd.clone.sunk | while | flops 155201664 | bytes 6544577 | solution.py:94
  15.1 9.7 %collective-permute-done = bf16[384,256]{1,0:T(8,128)(2,1)S(1)} collective-permute-done((bf16[384,256]{1,0:T(8,128)(2,1)S(1)}, bf16[384,256]{1,0:T(8,128)(2,1)S(1)}, u32[]{:S(2)}, u32[]{:S(2)}) %collective-permute-start) | collective-permute-done | bytes 196640 | tf_op jit(solution)/shard_map/while/body/eval_jaxpr/ppermute | solution.py:12
  28.5 10.2 %collective-permute-done = bf16[384,256]{1,0:T(8,128)(2,1)S(1)} collective-permute-done((bf16[384,256]{1,0:T(8,128)(2,1)S(1)}, bf16[384,256]{1,0:T(8,128)(2,1)S(1)}, u32[]{:S(2)}, u32[]{:S(2)}) %collective-permute-start) | collective-permute-done | bytes 196640 | tf_op jit(solution)/shard_map/while/body/eval_jaxpr/ppermute | solution.py:12
  42.3 9.5 %collective-permute-done = bf16[384,256]{1,0:T(8,128)(2,1)S(1)} collective-permute-done((bf16[384,256]{1,0:T(8,128)(2,1)S(1)}, bf16[384,256]{1,0:T(8,128)(2,1)S(1)}, u32[]{:S(2)}, u32[]{:S(2)}) %collective-permute-start) | collective-permute-done | bytes 196640 | tf_op jit(solution)/shard_map/while/body/eval_jaxpr/ppermute | solution.py:12
  134.3 9.9 %collective-permute-done = bf16[384,256]{1,0:T(8,128)(2,1)S(1)} collective-permute-done((bf16[384,256]{1,0:T(8,128)(2,1)S(1)}, bf16[384,256]{1,0:T(8,128)(2,1)S(1)}, u32[]{:S(2)}, u32[]{:S(2)}) %collective-permute-start) | collective-permute-done | bytes 196640 | tf_op jit(solution)/shard_map/while/body/eval_jaxpr/ppermute | solution.py:12
  147.9 11.2 %collective-permute-done = bf16[384,256]{1,0:T(8,128)(2,1)S(1)} collective-permute-done((bf16[384,256]{1,0:T(8,128)(2,1)S(1)}, bf16[384,256]{1,0:T(8,128)(2,1)S(1)}, u32[]{:S(2)}, u32[]{:S(2)}) %collective-permute-start) | collective-permute-done | bytes 196640 | tf_op jit(solution)/shard_map/while/body/eval_jaxpr/ppermute | solution.py:12
  162.7 10.9 %collective-permute-done = bf16[384,256]{1,0:T(8,128)(2,1)S(1)} collective-permute-done((bf16[384,256]{1,0:T(8,128)(2,1)S(1)}, bf16[384,256]{1,0:T(8,128)(2,1)S(1)}, u32[]{:S(2)}, u32[]{:S(2)}) %collective-permute-start) | collective-permute-done | bytes 196640 | tf_op jit(solution)/shard_map/while/body/eval_jaxpr/ppermute | solution.py:12
  177.2 10.1 %collective-permute-done = bf16[384,256]{1,0:T(8,128)(2,1)S(1)} collective-permute-done((bf16[384,256]{1,0:T(8,128)(2,1)S(1)}, bf16[384,256]{1,0:T(8,128)(2,1)S(1)}, u32[]{:S(2)}, u32[]{:S(2)}) %collective-permute-start) | collective-permute-done | bytes 196640 | tf_op jit(solution)/shard_map/while/body/eval_jaxpr/ppermute | solution.py:12
  282.9 10.0 %collective-permute-done = bf16[384,256]{1,0:T(8,128)(2,1)S(1)} collective-permute-done((bf16[384,256]{1,0:T(8,128)(2,1)S(1)}, bf16[384,256]{1,0:T(8,128)(2,1)S(1)}, u32[]{:S(2)}, u32[]{:S(2)}) %collective-permute-start) | collective-permute-done | bytes 196640 | tf_op jit(solution)/shard_map/while/body/eval_jaxpr/ppermute | solution.py:12
  296.6 11.3 %collective-permute-done = bf16[384,256]{1,0:T(8,128)(2,1)S(1)} collective-permute-done((bf16[384,256]{1,0:T(8,128)(2,1)S(1)}, bf16[384,256]{1,0:T(8,128)(2,1)S(1)}, u32[]{:S(2)}, u32[]{:S(2)}) %collective-permute-start) | collective-permute-done | bytes 196640 | tf_op jit(solution)/shard_map/while/body/eval_jaxpr/ppermute | solution.py:12
  311.5 10.8 %collective-permute-done = bf16[384,256]{1,0:T(8,128)(2,1)S(1)} collective-permute-done((bf16[384,256]{1,0:T(8,128)(2,1)S(1)}, bf16[384,256]{1,0:T(8,128)(2,1)S(1)}, u32[]{:S(2)}, u32[]{:S(2)}) %collective-permute-start) | collective-permute-done | bytes 196640 | tf_op jit(solution)/shard_map/while/body/eval_jaxpr/ppermute | solution.py:12
  325.9 10.0 %collective-permute-done = bf16[384,256]{1,0:T(8,128)(2,1)S(1)} collective-permute-done((bf16[384,256]{1,0:T(8,128)(2,1)S(1)}, bf16[384,256]{1,0:T(8,128)(2,1)S(1)}, u32[]{:S(2)}, u32[]{:S(2)}) %collective-permute-start) | collective-permute-done | bytes 196640 | tf_op jit(solution)/shard_map/while/body/eval_jaxpr/ppermute | solution.py:12
  431.5 10.2 %collective-permute-done = bf16[384,256]{1,0:T(8,128)(2,1)S(1)} collective-permute-done((bf16[384,256]{1,0:T(8,128)(2,1)S(1)}, bf16[384,256]{1,0:T(8,128)(2,1)S(1)}, u32[]{:S(2)}, u32[]{:S(2)}) %collective-permute-start) | collective-permute-done | bytes 196640 | tf_op jit(solution)/shard_map/while/body/eval_jaxpr/ppermute | solution.py:12
  445.3 11.3 %collective-permute-done = bf16[384,256]{1,0:T(8,128)(2,1)S(1)} collective-permute-done((bf16[384,256]{1,0:T(8,128)(2,1)S(1)}, bf16[384,256]{1,0:T(8,128)(2,1)S(1)}, u32[]{:S(2)}, u32[]{:S(2)}) %collective-permute-start) | collective-permute-done | bytes 196640 | tf_op jit(solution)/shard_map/while/body/eval_jaxpr/ppermute | solution.py:12
  460.3 10.7 %collective-permute-done = bf16[384,256]{1,0:T(8,128)(2,1)S(1)} collective-permute-done((bf16[384,256]{1,0:T(8,128)(2,1)S(1)}, bf16[384,256]{1,0:T(8,128)(2,1)S(1)}, u32[]{:S(2)}, u32[]{:S(2)}) %collective-permute-start) | collective-permute-done | bytes 196640 | tf_op jit(solution)/shard_map/while/body/eval_jaxpr/ppermute | solution.py:12
  474.7 9.9 %collective-permute-done = bf16[384,256]{1,0:T(8,128)(2,1)S(1)} collective-permute-done((bf16[384,256]{1,0:T(8,128)(2,1)S(1)}, bf16[384,256]{1,0:T(8,128)(2,1)S(1)}, u32[]{:S(2)}, u32[]{:S(2)}) %collective-permute-start) | collective-permute-done | bytes 196640 | tf_op jit(solution)/shard_map/while/body/eval_jaxpr/ppermute | solution.py:12
  580.2 10.2 %collective-permute-done = bf16[384,256]{1,0:T(8,128)(2,1)S(1)} collective-permute-done((bf16[384,256]{1,0:T(8,128)(2,1)S(1)}, bf16[384,256]{1,0:T(8,128)(2,1)S(1)}, u32[]{:S(2)}, u32[]{:S(2)}) %collective-permute-start) | collective-permute-done | bytes 196640 | tf_op jit(solution)/shard_map/while/body/eval_jaxpr/ppermute | solution.py:12
  594.1 11.4 %collective-permute-done = bf16[384,256]{1,0:T(8,128)(2,1)S(1)} collective-permute-done((bf16[384,256]{1,0:T(8,128)(2,1)S(1)}, bf16[384,256]{1,0:T(8,128)(2,1)S(1)}, u32[]{:S(2)}, u32[]{:S(2)}) %collective-permute-start) | collective-permute-done | bytes 196640 | tf_op jit(solution)/shard_map/while/body/eval_jaxpr/ppermute | solution.py:12
  609.1 10.7 %collective-permute-done = bf16[384,256]{1,0:T(8,128)(2,1)S(1)} collective-permute-done((bf16[384,256]{1,0:T(8,128)(2,1)S(1)}, bf16[384,256]{1,0:T(8,128)(2,1)S(1)}, u32[]{:S(2)}, u32[]{:S(2)}) %collective-permute-start) | collective-permute-done | bytes 196640 | tf_op jit(solution)/shard_map/while/body/eval_jaxpr/ppermute | solution.py:12
  623.5 9.9 %collective-permute-done = bf16[384,256]{1,0:T(8,128)(2,1)S(1)} collective-permute-done((bf16[384,256]{1,0:T(8,128)(2,1)S(1)}, bf16[384,256]{1,0:T(8,128)(2,1)S(1)}, u32[]{:S(2)}, u32[]{:S(2)}) %collective-permute-start) | collective-permute-done | bytes 196640 | tf_op jit(solution)/shard_map/while/body/eval_jaxpr/ppermute | solution.py:12
  729.0 10.2 %collective-permute-done = bf16[384,256]{1,0:T(8,128)(2,1)S(1)} collective-permute-done((bf16[384,256]{1,0:T(8,128)(2,1)S(1)}, bf16[384,256]{1,0:T(8,128)(2,1)S(1)}, u32[]{:S(2)}, u32[]{:S(2)}) %collective-permute-start) | collective-permute-done | bytes 196640 | tf_op jit(solution)/shard_map/while/body/eval_jaxpr/ppermute | solution.py:12
  742.9 11.4 %collective-permute-done = bf16[384,256]{1,0:T(8,128)(2,1)S(1)} collective-permute-done((bf16[384,256]{1,0:T(8,128)(2,1)S(1)}, bf16[384,256]{1,0:T(8,128)(2,1)S(1)}, u32[]{:S(2)}, u32[]{:S(2)}) %collective-permute-start) | collective-permute-done | bytes 196640 | tf_op jit(solution)/shard_map/while/body/eval_jaxpr/ppermute | solution.py:12
  757.9 10.7 %collective-permute-done = bf16[384,256]{1,0:T(8,128)(2,1)S(1)} collective-permute-done((bf16[384,256]{1,0:T(8,128)(2,1)S(1)}, bf16[384,256]{1,0:T(8,128)(2,1)S(1)}, u32[]{:S(2)}, u32[]{:S(2)}) %collective-permute-start) | collective-permute-done | bytes 196640 | tf_op jit(solution)/shard_map/while/body/eval_jaxpr/ppermute | solution.py:12
  772.3 9.9 %collective-permute-done = bf16[384,256]{1,0:T(8,128)(2,1)S(1)} collective-permute-done((bf16[384,256]{1,0:T(8,128)(2,1)S(1)}, bf16[384,256]{1,0:T(8,128)(2,1)S(1)}, u32[]{:S(2)}, u32[]{:S(2)}) %collective-permute-start) | collective-permute-done | bytes 196640 | tf_op jit(solution)/shard_map/while/body/eval_jaxpr/ppermute | solution.py:12
  (686 shorter events, 618.7 us)
Async XLA Ops:
  11.6 13.3 %collective-permute-start = (bf16[384,256]{1,0:T(8,128)(2,1)S(1)}, bf16[384,256]{1,0:T(8,128)(2,1)S(1)}, u32[]{:S(2)}, u32[]{:S(2)}) collective-permute-start(bf16[384,256]{1,0:T(8,128)(2,1)S(1)} %get-tuple-element.344), channel_id=1, source_target_pairs={{0,4},{4,8},{8,12},{12,16},{16,20},{20,24},{24,28},{28,32},{32,36}... | collective-permute-start | bytes 589832 | tf_op jit(solution)/shard_map/while/body/eval_jaxpr/ppermute | solution.py:12
  26.2 12.5 %collective-permute-start = (bf16[384,256]{1,0:T(8,128)(2,1)S(1)}, bf16[384,256]{1,0:T(8,128)(2,1)S(1)}, u32[]{:S(2)}, u32[]{:S(2)}) collective-permute-start(bf16[384,256]{1,0:T(8,128)(2,1)S(1)} %get-tuple-element.344), channel_id=1, source_target_pairs={{0,4},{4,8},{8,12},{12,16},{16,20},{20,24},{24,28},{28,32},{32,36}... | collective-permute-start | bytes 589832 | tf_op jit(solution)/shard_map/while/body/eval_jaxpr/ppermute | solution.py:12
  40.0 11.8 %collective-permute-start = (bf16[384,256]{1,0:T(8,128)(2,1)S(1)}, bf16[384,256]{1,0:T(8,128)(2,1)S(1)}, u32[]{:S(2)}, u32[]{:S(2)}) collective-permute-start(bf16[384,256]{1,0:T(8,128)(2,1)S(1)} %get-tuple-element.344), channel_id=1, source_target_pairs={{0,4},{4,8},{8,12},{12,16},{16,20},{20,24},{24,28},{28,32},{32,36}... | collective-permute-start | bytes 589832 | tf_op jit(solution)/shard_map/while/body/eval_jaxpr/ppermute | solution.py:12
  53.2 11.8 %collective-permute-start = (bf16[384,256]{1,0:T(8,128)(2,1)S(1)}, bf16[384,256]{1,0:T(8,128)(2,1)S(1)}, u32[]{:S(2)}, u32[]{:S(2)}) collective-permute-start(bf16[384,256]{1,0:T(8,128)(2,1)S(1)} %get-tuple-element.344), channel_id=1, source_target_pairs={{0,4},{4,8},{8,12},{12,16},{16,20},{20,24},{24,28},{28,32},{32,36}... | collective-permute-start | bytes 589832 | tf_op jit(solution)/shard_map/while/body/eval_jaxpr/ppermute | solution.py:12
  132.0 12.2 %collective-permute-start = (bf16[384,256]{1,0:T(8,128)(2,1)S(1)}, bf16[384,256]{1,0:T(8,128)(2,1)S(1)}, u32[]{:S(2)}, u32[]{:S(2)}) collective-permute-start(bf16[384,256]{1,0:T(8,128)(2,1)S(1)} %get-tuple-element.344), channel_id=1, source_target_pairs={{0,4},{4,8},{8,12},{12,16},{16,20},{20,24},{24,28},{28,32},{32,36}... | collective-permute-start | bytes 589832 | tf_op jit(solution)/shard_map/while/body/eval_jaxpr/ppermute | solution.py:12
  145.6 13.5 %collective-permute-start = (bf16[384,256]{1,0:T(8,128)(2,1)S(1)}, bf16[384,256]{1,0:T(8,128)(2,1)S(1)}, u32[]{:S(2)}, u32[]{:S(2)}) collective-permute-start(bf16[384,256]{1,0:T(8,128)(2,1)S(1)} %get-tuple-element.344), channel_id=1, source_target_pairs={{0,4},{4,8},{8,12},{12,16},{16,20},{20,24},{24,28},{28,32},{32,36}... | collective-permute-start | bytes 589832 | tf_op jit(solution)/shard_map/while/body/eval_jaxpr/ppermute | solution.py:12
  160.4 13.2 %collective-permute-start = (bf16[384,256]{1,0:T(8,128)(2,1)S(1)}, bf16[384,256]{1,0:T(8,128)(2,1)S(1)}, u32[]{:S(2)}, u32[]{:S(2)}) collective-permute-start(bf16[384,256]{1,0:T(8,128)(2,1)S(1)} %get-tuple-element.344), channel_id=1, source_target_pairs={{0,4},{4,8},{8,12},{12,16},{16,20},{20,24},{24,28},{28,32},{32,36}... | collective-permute-start | bytes 589832 | tf_op jit(solution)/shard_map/while/body/eval_jaxpr/ppermute | solution.py:12
  174.9 12.4 %collective-permute-start = (bf16[384,256]{1,0:T(8,128)(2,1)S(1)}, bf16[384,256]{1,0:T(8,128)(2,1)S(1)}, u32[]{:S(2)}, u32[]{:S(2)}) collective-permute-start(bf16[384,256]{1,0:T(8,128)(2,1)S(1)} %get-tuple-element.344), channel_id=1, source_target_pairs={{0,4},{4,8},{8,12},{12,16},{16,20},{20,24},{24,28},{28,32},{32,36}... | collective-permute-start | bytes 589832 | tf_op jit(solution)/shard_map/while/body/eval_jaxpr/ppermute | solution.py:12
  280.6 12.3 %collective-permute-start = (bf16[384,256]{1,0:T(8,128)(2,1)S(1)}, bf16[384,256]{1,0:T(8,128)(2,1)S(1)}, u32[]{:S(2)}, u32[]{:S(2)}) collective-permute-start(bf16[384,256]{1,0:T(8,128)(2,1)S(1)} %get-tuple-element.344), channel_id=1, source_target_pairs={{0,4},{4,8},{8,12},{12,16},{16,20},{20,24},{24,28},{28,32},{32,36}... | collective-permute-start | bytes 589832 | tf_op jit(solution)/shard_map/while/body/eval_jaxpr/ppermute | solution.py:12
  294.3 13.6 %collective-permute-start = (bf16[384,256]{1,0:T(8,128)(2,1)S(1)}, bf16[384,256]{1,0:T(8,128)(2,1)S(1)}, u32[]{:S(2)}, u32[]{:S(2)}) collective-permute-start(bf16[384,256]{1,0:T(8,128)(2,1)S(1)} %get-tuple-element.344), channel_id=1, source_target_pairs={{0,4},{4,8},{8,12},{12,16},{16,20},{20,24},{24,28},{28,32},{32,36}... | collective-permute-start | bytes 589832 | tf_op jit(solution)/shard_map/while/body/eval_jaxpr/ppermute | solution.py:12
  309.2 13.1 %collective-permute-start = (bf16[384,256]{1,0:T(8,128)(2,1)S(1)}, bf16[384,256]{1,0:T(8,128)(2,1)S(1)}, u32[]{:S(2)}, u32[]{:S(2)}) collective-permute-start(bf16[384,256]{1,0:T(8,128)(2,1)S(1)} %get-tuple-element.344), channel_id=1, source_target_pairs={{0,4},{4,8},{8,12},{12,16},{16,20},{20,24},{24,28},{28,32},{32,36}... | collective-permute-start | bytes 589832 | tf_op jit(solution)/shard_map/while/body/eval_jaxpr/ppermute | solution.py:12
  323.7 12.2 %collective-permute-start = (bf16[384,256]{1,0:T(8,128)(2,1)S(1)}, bf16[384,256]{1,0:T(8,128)(2,1)S(1)}, u32[]{:S(2)}, u32[]{:S(2)}) collective-permute-start(bf16[384,256]{1,0:T(8,128)(2,1)S(1)} %get-tuple-element.344), channel_id=1, source_target_pairs={{0,4},{4,8},{8,12},{12,16},{16,20},{20,24},{24,28},{28,32},{32,36}... | collective-permute-start | bytes 589832 | tf_op jit(solution)/shard_map/while/body/eval_jaxpr/ppermute | solution.py:12
  429.2 12.5 %collective-permute-start = (bf16[384,256]{1,0:T(8,128)(2,1)S(1)}, bf16[384,256]{1,0:T(8,128)(2,1)S(1)}, u32[]{:S(2)}, u32[]{:S(2)}) collective-permute-start(bf16[384,256]{1,0:T(8,128)(2,1)S(1)} %get-tuple-element.344), channel_id=1, source_target_pairs={{0,4},{4,8},{8,12},{12,16},{16,20},{20,24},{24,28},{28,32},{32,36}... | collective-permute-start | bytes 589832 | tf_op jit(solution)/shard_map/while/body/eval_jaxpr/ppermute | solution.py:12
  443.0 13.6 %collective-permute-start = (bf16[384,256]{1,0:T(8,128)(2,1)S(1)}, bf16[384,256]{1,0:T(8,128)(2,1)S(1)}, u32[]{:S(2)}, u32[]{:S(2)}) collective-permute-start(bf16[384,256]{1,0:T(8,128)(2,1)S(1)} %get-tuple-element.344), channel_id=1, source_target_pairs={{0,4},{4,8},{8,12},{12,16},{16,20},{20,24},{24,28},{28,32},{32,36}... | collective-permute-start | bytes 589832 | tf_op jit(solution)/shard_map/while/body/eval_jaxpr/ppermute | solution.py:12
  458.0 13.0 %collective-permute-start = (bf16[384,256]{1,0:T(8,128)(2,1)S(1)}, bf16[384,256]{1,0:T(8,128)(2,1)S(1)}, u32[]{:S(2)}, u32[]{:S(2)}) collective-permute-start(bf16[384,256]{1,0:T(8,128)(2,1)S(1)} %get-tuple-element.344), channel_id=1, source_target_pairs={{0,4},{4,8},{8,12},{12,16},{16,20},{20,24},{24,28},{28,32},{32,36}... | collective-permute-start | bytes 589832 | tf_op jit(solution)/shard_map/while/body/eval_jaxpr/ppermute | solution.py:12
  472.4 12.2 %collective-permute-start = (bf16[384,256]{1,0:T(8,128)(2,1)S(1)}, bf16[384,256]{1,0:T(8,128)(2,1)S(1)}, u32[]{:S(2)}, u32[]{:S(2)}) collective-permute-start(bf16[384,256]{1,0:T(8,128)(2,1)S(1)} %get-tuple-element.344), channel_id=1, source_target_pairs={{0,4},{4,8},{8,12},{12,16},{16,20},{20,24},{24,28},{28,32},{32,36}... | collective-permute-start | bytes 589832 | tf_op jit(solution)/shard_map/while/body/eval_jaxpr/ppermute | solution.py:12
  577.9 12.5 %collective-permute-start = (bf16[384,256]{1,0:T(8,128)(2,1)S(1)}, bf16[384,256]{1,0:T(8,128)(2,1)S(1)}, u32[]{:S(2)}, u32[]{:S(2)}) collective-permute-start(bf16[384,256]{1,0:T(8,128)(2,1)S(1)} %get-tuple-element.344), channel_id=1, source_target_pairs={{0,4},{4,8},{8,12},{12,16},{16,20},{20,24},{24,28},{28,32},{32,36}... | collective-permute-start | bytes 589832 | tf_op jit(solution)/shard_map/while/body/eval_jaxpr/ppermute | solution.py:12
  591.8 13.7 %collective-permute-start = (bf16[384,256]{1,0:T(8,128)(2,1)S(1)}, bf16[384,256]{1,0:T(8,128)(2,1)S(1)}, u32[]{:S(2)}, u32[]{:S(2)}) collective-permute-start(bf16[384,256]{1,0:T(8,128)(2,1)S(1)} %get-tuple-element.344), channel_id=1, source_target_pairs={{0,4},{4,8},{8,12},{12,16},{16,20},{20,24},{24,28},{28,32},{32,36}... | collective-permute-start | bytes 589832 | tf_op jit(solution)/shard_map/while/body/eval_jaxpr/ppermute | solution.py:12
  606.8 13.0 %collective-permute-start = (bf16[384,256]{1,0:T(8,128)(2,1)S(1)}, bf16[384,256]{1,0:T(8,128)(2,1)S(1)}, u32[]{:S(2)}, u32[]{:S(2)}) collective-permute-start(bf16[384,256]{1,0:T(8,128)(2,1)S(1)} %get-tuple-element.344), channel_id=1, source_target_pairs={{0,4},{4,8},{8,12},{12,16},{16,20},{20,24},{24,28},{28,32},{32,36}... | collective-permute-start | bytes 589832 | tf_op jit(solution)/shard_map/while/body/eval_jaxpr/ppermute | solution.py:12
  621.2 12.2 %collective-permute-start = (bf16[384,256]{1,0:T(8,128)(2,1)S(1)}, bf16[384,256]{1,0:T(8,128)(2,1)S(1)}, u32[]{:S(2)}, u32[]{:S(2)}) collective-permute-start(bf16[384,256]{1,0:T(8,128)(2,1)S(1)} %get-tuple-element.344), channel_id=1, source_target_pairs={{0,4},{4,8},{8,12},{12,16},{16,20},{20,24},{24,28},{28,32},{32,36}... | collective-permute-start | bytes 589832 | tf_op jit(solution)/shard_map/while/body/eval_jaxpr/ppermute | solution.py:12
  726.7 12.5 %collective-permute-start = (bf16[384,256]{1,0:T(8,128)(2,1)S(1)}, bf16[384,256]{1,0:T(8,128)(2,1)S(1)}, u32[]{:S(2)}, u32[]{:S(2)}) collective-permute-start(bf16[384,256]{1,0:T(8,128)(2,1)S(1)} %get-tuple-element.344), channel_id=1, source_target_pairs={{0,4},{4,8},{8,12},{12,16},{16,20},{20,24},{24,28},{28,32},{32,36}... | collective-permute-start | bytes 589832 | tf_op jit(solution)/shard_map/while/body/eval_jaxpr/ppermute | solution.py:12
  740.6 13.7 %collective-permute-start = (bf16[384,256]{1,0:T(8,128)(2,1)S(1)}, bf16[384,256]{1,0:T(8,128)(2,1)S(1)}, u32[]{:S(2)}, u32[]{:S(2)}) collective-permute-start(bf16[384,256]{1,0:T(8,128)(2,1)S(1)} %get-tuple-element.344), channel_id=1, source_target_pairs={{0,4},{4,8},{8,12},{12,16},{16,20},{20,24},{24,28},{28,32},{32,36}... | collective-permute-start | bytes 589832 | tf_op jit(solution)/shard_map/while/body/eval_jaxpr/ppermute | solution.py:12
  755.6 13.0 %collective-permute-start = (bf16[384,256]{1,0:T(8,128)(2,1)S(1)}, bf16[384,256]{1,0:T(8,128)(2,1)S(1)}, u32[]{:S(2)}, u32[]{:S(2)}) collective-permute-start(bf16[384,256]{1,0:T(8,128)(2,1)S(1)} %get-tuple-element.344), channel_id=1, source_target_pairs={{0,4},{4,8},{8,12},{12,16},{16,20},{20,24},{24,28},{28,32},{32,36}... | collective-permute-start | bytes 589832 | tf_op jit(solution)/shard_map/while/body/eval_jaxpr/ppermute | solution.py:12
  770.0 12.2 %collective-permute-start = (bf16[384,256]{1,0:T(8,128)(2,1)S(1)}, bf16[384,256]{1,0:T(8,128)(2,1)S(1)}, u32[]{:S(2)}, u32[]{:S(2)}) collective-permute-start(bf16[384,256]{1,0:T(8,128)(2,1)S(1)} %get-tuple-element.344), channel_id=1, source_target_pairs={{0,4},{4,8},{8,12},{12,16},{16,20},{20,24},{24,28},{28,32},{32,36}... | collective-permute-start | bytes 589832 | tf_op jit(solution)/shard_map/while/body/eval_jaxpr/ppermute | solution.py:12
  (39 other events, 459.5 us)
where the time goes:
time: 865 us; the launch traced here: 863 us
  waiting for transfers between devices  620 us (72%)
  starting transfers between devices  122 us (14%)
  matrix products  66.2 us (8%)
  other arithmetic  40.6 us (5%)
    ppermute x63, waiting for transfers between devices, passed_along(): return lax.ppermute(shard, axis, pairs)  620 us
    ppermute x63, starting transfers between devices, passed_along(): return lax.ppermute(shard, axis, pairs)  122 us
    dot_general x64, matrix products, block_terms(): jnp.einsum('qhk,kd->qhd', weights, value_block, preferred_element_type=jn...  42.7 us
    dot_general x64, matrix products, block_terms(): jnp.einsum('qhd,kd->qhk', query_heads, key_block, preferred_element_type=...  23.5 us
  transfers between devices with their start and end apart: 63, of which 63 were waited for; matrix products, arithmetic and copies ran while one was open for 2% of the time, Pallas kernels for 0%

commit v1 on v0

v1 whole, which is shorter than its diff:
```python
import functools
import math

import jax
import jax.numpy as jnp
from jax import lax
from jax.experimental import pallas as pl
from jax.experimental.pallas import tpu as pltpu
from jax.sharding import PartitionSpec as P

NEG = -1e30
FAR = -(1 << 20)

NZ, NX, NY, NC = 8, 4, 4, 2
PAIRS = NZ * NX

WIDE = 8
LAST = 8


def device_index(pair, y, core):
    z, x = divmod(pair, NX)
    y = y % NY
    return (z * NX * 2 + x * 2 + y % 2) * 4 + (y // 2) * NC + core


def send(array, move):
    pairs = []
    for pair in range(PAIRS):
        for y in range(NY):
            for core in range(NC):
                target = move(pair, y, core)
                if target is not None:
                    pairs.append((device_index(pair, y, core), device_index(*target)))
    return lax.ppermute(array, ("ctx", "head"), sorted(pairs))


def later_plane(by):
    return lambda pair, y, core: ((pair + by * NX) % PAIRS, y, core)


def along_x(pair, by):
    return pair - pair % NX + (pair + by) % NX


def first_axis(by):
    return lambda pair, y, core: (along_x(pair, by), y, core) if core == 0 else (pair, y + by, core)


def second_axis(by):
    return lambda pair, y, core: (pair, y + by, core) if core == 0 else (along_x(pair, by), y, core)


def other_core(pair, y, core):
    return (pair, y, 1 - core)


def place(row_count, chunk):
    ctx = lax.axis_index("ctx")
    head = lax.axis_index("head")
    core, y_hi = head % NC, head // NC
    pair, y = ctx // 2, y_hi * 2 + ctx % 2

    def start_of(back, turn):
        there = (y - turn + NY) % NY
        return (2 * (pair - back) + there % 2) * row_count + (there // 2) * (NC * chunk) + core * chunk

    return ctx, core, y, start_of


def near_starts(core, start_of):
    return [jnp.where(core == 0, start_of(i, 0), start_of(i // NY * NX, i % NY)) for i in range(WIDE)]


def far_starts(core, start_of):
    return [start_of(LAST, 0)] + [jnp.where(core == 0, FAR, start_of(LAST, turn)) for turn in (1, 2, 3)]


def side_starts(core, y, start_of, by):
    skip = (y + by) % 2 if by != 2 else 0
    return [
        jnp.where(core == 0, start_of(i + skip, by), start_of(i // NY * NX + by, i % NY)) for i in range(WIDE)
    ]


def last_starts(core, start_of):
    return [jnp.where(core == 0, start_of(LAST, 2), FAR)]


def attend_kernel(names, groups, chunk, scale, opening, *refs):
    lens = refs[0]
    q_refs = refs[1 : 1 + groups]
    kv = dict(zip(names, refs[1 + groups :]))
    refs = refs[1 + groups + len(names) :]
    rows = q_refs[0].shape[0]
    head_dim = kv[names[0]].shape[1] // 2
    heads_here = q_refs[0].shape[1] // head_dim
    row_m, row_l = slice(head_dim, head_dim + 1), slice(head_dim + 1, head_dim + 2)
    state = refs if opening else refs[groups:]
    for group, ref in enumerate(state):
        if opening:
            ref[...] = jnp.zeros(ref.shape, jnp.float32)
            ref[row_m, :] = jnp.full((1, ref.shape[1]), NEG, jnp.float32)
        else:
            ref[...] = refs[group][...]

    ctx, core, y, start_of = place(rows, chunk)
    first_row = ctx * rows
    last_row = first_row + (rows - 1)
    q_pos = first_row + lax.broadcasted_iota(jnp.int32, (1, rows), 1)
    end = jnp.int32(0)
    first_doc = last_doc = jnp.int32(0)
    doc_start = jnp.zeros((1, rows), jnp.int32)
    for i in range(lens.shape[0]):
        end = end + lens[i]
        doc_start = jnp.where(end <= q_pos, end, doc_start)
        first_doc = jnp.where(end <= first_row, end, first_doc)
        last_doc = jnp.where(end <= last_row, end, last_doc)

    def absorb(tile, starts, masked):
        keys = len(starts) * chunk
        key_tile = tile[:, :head_dim]
        value_t = jnp.concatenate([tile[:, head_dim:].T, jnp.ones((16, keys), tile.dtype)], axis=0)
        if masked:
            step = lax.broadcasted_iota(jnp.int32, (chunk, 1), 0)
            past = jnp.concatenate([step + start for start in starts], axis=0) - doc_start
            reach = (q_pos - doc_start).astype(jnp.uint32)
            allowed = past.astype(jnp.uint32) <= reach

        def scores(group, h):
            return lax.dot_general(
                key_tile,
                q_refs[group][:, h * head_dim : (h + 1) * head_dim],
                (((1,), (1,)), ((), ())),
                preferred_element_type=jnp.float32,
            )

        def finish(group, h, p, alpha):
            ref, cols = state[group], slice(h * rows, (h + 1) * rows)
            out = jnp.dot(value_t, p, preferred_element_type=jnp.float32)
            ref[row_l, cols] = ref[row_l, cols] * alpha + out[head_dim : head_dim + 1]
            ref[:head_dim, cols] = ref[:head_dim, cols] * alpha + out[:head_dim]

        heads = [(group, h) for group in range(groups) for h in range(heads_here)]
        ahead = [scores(*heads[0]), scores(*heads[1])]
        waiting = None
        for j, (group, h) in enumerate(heads):
            ref, cols = state[group], slice(h * rows, (h + 1) * rows)
            s = ahead.pop(0)
            if j + 2 < len(heads):
                ahead.append(scores(*heads[j + 2]))
            if masked:
                s = jnp.where(allowed, s, NEG)
            m_old = ref[row_m, cols]
            m_new = jnp.maximum(m_old, jnp.max(s, axis=0, keepdims=True))
            alpha = jnp.exp2((m_old - m_new) * scale)
            p = jnp.exp2((s - m_new) * scale).astype(jnp.bfloat16)
            ref[row_m, cols] = m_new
            if waiting is not None:
                finish(*waiting)
            waiting = (group, h, p, alpha)
        finish(*waiting)

    def absorb_if_needed(load, starts):
        needed = full = None
        for start in starts:
            here = (start + (chunk - 1) >= first_doc) & (start <= last_row)
            whole = (start >= last_doc) & (start + (chunk - 1) <= first_row)
            needed = here if needed is None else needed | here
            full = whole if full is None else full & whole

        @pl.when(full)
        def _():
            absorb(load(), starts, False)

        @pl.when(needed & jnp.logical_not(full))
        def _():
            absorb(load(), starts, True)

    wide = WIDE * chunk
    if "own" in kv:
        absorb_if_needed(lambda: kv["own"][:wide, :], near_starts(core, start_of))
        absorb_if_needed(lambda: kv["own"][wide : wide + NY * chunk, :], far_starts(core, start_of))
    for by in (1, 3, 2):
        if by in kv:
            absorb_if_needed(lambda by=by: kv[by][:wide, :], side_starts(core, y, start_of, by))
    if 2 in kv:
        absorb_if_needed(lambda: kv[2][wide:, :], last_starts(core, start_of))


def attend(lens, qs, kv, states, chunk, head_dim, scale):
    smem = pl.BlockSpec(memory_space=pltpu.SMEM)
    vmem = pl.BlockSpec(memory_space=pltpu.VMEM)
    rows = qs[0].shape[0] * (qs[0].shape[1] // head_dim)
    names, arrays = tuple(kv), list(kv.values())
    keys = sum(array.shape[0] for array in arrays)
    given = list(states or [])
    return pl.pallas_call(
        functools.partial(attend_kernel, names, len(qs), chunk, scale, states is None),
        out_shape=[jax.ShapeDtypeStruct((head_dim + 8, rows), jnp.float32)] * len(qs),
        in_specs=[smem] + [vmem] * (len(qs) + len(arrays) + len(given)),
        out_specs=[vmem] * len(qs),
        compiler_params=pltpu.CompilerParams(vmem_limit_bytes=32 * 1024 * 1024),
        cost_estimate=pl.CostEstimate(
            flops=4 * keys * rows * len(qs) * head_dim,
            bytes_accessed=4 * rows * head_dim,
            transcendentals=keys * rows * len(qs),
        ),
    )(lens, *qs, *arrays, *given)


def join_kernel(k_ref, v_ref, out_ref, sems):
    head_dim = k_ref.shape[1]
    copies = [
        pltpu.make_async_copy(k_ref, out_ref.at[:, :head_dim], sems.at[0]),
        pltpu.make_async_copy(v_ref, out_ref.at[:, head_dim:], sems.at[1]),
    ]
    for copy in copies:
        copy.start()
    for copy in copies:
        copy.wait()


def join(key_rows, value_rows):
    chunk, head_dim = key_rows.shape
    return pl.pallas_call(
        join_kernel,
        out_shape=jax.ShapeDtypeStruct((chunk, 2 * head_dim), key_rows.dtype),
        in_specs=[pl.BlockSpec(memory_space=pltpu.HBM)] * 2,
        out_specs=pl.BlockSpec(memory_space=pltpu.VMEM),
        scratch_shapes=[pltpu.SemaphoreType.DMA((2,))],
        compiler_params=pltpu.CompilerParams(vmem_limit_bytes=4 * 1024 * 1024),
    )(key_rows, value_rows)


def merge_kernel(head_dim, scale, keep_ref, came_ref, out_ref):
    rows = out_ref.shape[0]
    for h in range(out_ref.shape[1] // head_dim):
        cols = slice(h * rows, (h + 1) * rows)
        m_a, m_b = keep_ref[head_dim : head_dim + 1, cols], came_ref[head_dim : head_dim + 1, cols]
        l_a, l_b = keep_ref[head_dim + 1 : head_dim + 2, cols], came_ref[head_dim + 1 : head_dim + 2, cols]
        top = jnp.maximum(m_a, m_b)
        w_a, w_b = jnp.exp2((m_a - top) * scale), jnp.exp2((m_b - top) * scale)
        total = l_a * w_a + l_b * w_b
        w_a, w_b = w_a / total, w_b / total
        result = keep_ref[:head_dim, cols] * w_a + came_ref[:head_dim, cols] * w_b
        out_ref[:, h * head_dim : (h + 1) * head_dim] = result.T.astype(out_ref.dtype)


def merge(keep, came, rows, head_dim, scale):
    vmem = pl.BlockSpec(memory_space=pltpu.VMEM)
    heads = keep.shape[1] // rows
    return pl.pallas_call(
        functools.partial(merge_kernel, head_dim, scale),
        out_shape=jax.ShapeDtypeStruct((rows, heads * head_dim), jnp.bfloat16),
        in_specs=[vmem, vmem],
        out_specs=vmem,
        compiler_params=pltpu.CompilerParams(vmem_limit_bytes=8 * 1024 * 1024),
    )(keep, came)


def on_device(queries, key_rows, value_rows, doc_lengths):
    row_count = queries.shape[0]
    chunk, head_dim = key_rows.shape
    scale = math.log2(math.e) / math.sqrt(head_dim)
    ctx = lax.axis_index("ctx")
    core = lax.axis_index("head") % NC

    own = join(key_rows, value_rows)
    back8 = send(own, later_plane(2))
    back4 = send(own, later_plane(1))
    own, back4, back8, late_q = lax.optimization_barrier((own, back4, back8, queries))
    other_q = send(late_q, other_core)

    def round_x(by):
        return (ctx // 2) % NX + by >= NX

    def first(by):
        wraps = (core == 0) & round_x(by)
        parts = [jnp.where(wraps, back4, own), jnp.where(wraps, back8, back4), back8]
        return send(jnp.concatenate(parts, axis=0), first_axis(by))

    got = {by: first(by) for by in (1, 3, 2)}
    planes = [own, back4, back8]
    held = []
    for i, plane in enumerate(planes):
        held += [plane] + [got[by][i * chunk : (i + 1) * chunk] for by in (1, 2, 3)]
    held = jnp.concatenate(held + [own], axis=0)

    def second(by, chunks):
        begin = jnp.where(core == 0, ctx % 2 if by != 2 else 0, jnp.where(round_x(by), NY, 0))
        return send(lax.dynamic_slice_in_dim(held, begin * chunk, chunks * chunk, 0), second_axis(by))

    b1, b3 = second(1, WIDE), second(3, WIDE)
    call = functools.partial(attend, doc_lengths, chunk=chunk, head_dim=head_dim, scale=scale)
    both = [queries, other_q]
    states = call(both, {"own": held}, None)
    held, *states = lax.optimization_barrier((held, *states))
    b2 = second(2, WIDE + 1)
    states = call(both, {1: b1}, states)
    keep, away = call(both, {3: b3}, states)
    (away,) = call([other_q], {2: b2}, [away])
    came = send(away, other_core)
    (keep,) = call([queries], {2: b2}, [keep])
    return merge(keep, came, row_count, head_dim, scale)


def solution(mesh):
    return jax.shard_map(
        on_device,
        mesh=mesh,
        in_specs=(P("ctx", "head"), P(("ctx", "head"), None), P(("ctx", "head"), None), P()),
        out_specs=P("ctx", "head"),
        check_vma=False,
    )
```

time: 865 us -> 44.1 us (0.05)
  the two profiles are of different devices: /device:TPU:144 before, /device:TPU:1 now
where the time goes in v1:
time: 44.1 us; the launch traced here: 43.9 us
  starting transfers between devices  18.4 us (42%)
  waiting for transfers between devices  16.8 us (38%)
  Pallas kernels  6.83 us (15%)
  local copies, waits for them, and re-layouts  1.65 us (4%)
    ppermute x10, starting transfers between devices, send(): return lax.ppermute(array, ('ctx', 'head'), sorted(pairs))  18.4 us
    ppermute x10, waiting for transfers between devices, send(): return lax.ppermute(array, ('ctx', 'head'), sorted(pairs))  16.8 us
    pallas_call x5, Pallas kernels, attend(): pl.pallas_call(functools.partial(attend_kernel, names, len(qs), chunk, sc...  5.96 us
    unnamed x19, local copies, waits for them, and re-layouts  1.55 us
  transfers between devices with their start and end apart: 10, of which 7 were waited for; matrix products, arithmetic and copies ran while one was open for 0% of the time, Pallas kernels for 12%

profile of v1, /device:TPU:1, one launch (start us, length us, event | category | flops | bytes accessed | tf_op | source)
XLA Modules:
  0.0 43.9 jit_solution(6758744129203778109)
XLA Ops:
  0.0 0.7 %copy-done.1 = bf16[96,128]{1,0:T(8,128)(2,1)S(1)} copy-done((bf16[96,128]{1,0:T(8,128)(2,1)S(1)}, bf16[96,128]{1,0:T(8,128)(2,1)}, u32[]{:S(2)}) %copy-start.1) | copy-done | bytes 24600
  0.7 0.7 %copy-done.2 = bf16[96,128]{1,0:T(8,128)(2,1)S(1)} copy-done((bf16[96,128]{1,0:T(8,128)(2,1)S(1)}, bf16[96,128]{1,0:T(8,128)(2,1)}, u32[]{:S(2)}) %copy-start.2) | copy-done | bytes 24600
  1.5 3.9 %collective-permute-start.1 = (bf16[96,256]{1,0:T(8,128)(2,1)S(1)}, bf16[96,256]{1,0:T(8,128)(2,1)S(1)}, u32[]{:S(2)}, u32[]{:S(2)}) collective-permute-start(bf16[96,256]{1,0:T(8,128)(2,1)S(1)} %shard_map.46), channel_id=1, source_target_pairs={{0,64},{1,65},{2,66},{3,67},{4,68},{5,69},{6,70},{7,71},{8,72},{9,... | collective-permute-start | bytes 147464 | tf_op jit(solution)/shard_map/ppermute | solution.py:35
  5.4 1.6 %collective-permute-start = (bf16[96,256]{1,0:T(8,128)(2,1)S(1)}, bf16[96,256]{1,0:T(8,128)(2,1)S(1)}, u32[]{:S(2)}, u32[]{:S(2)}) collective-permute-start(bf16[96,256]{1,0:T(8,128)(2,1)S(1)} %shard_map.46), channel_id=1, source_target_pairs={{0,32},{1,33},{2,34},{3,35},{4,36},{5,37},{6,38},{7,39},{8,40},{9,... | collective-permute-start | bytes 147464 | tf_op jit(solution)/shard_map/ppermute | solution.py:35
  7.1 3.0 %collective-permute-done.1 = bf16[96,256]{1,0:T(8,128)(2,1)S(1)} collective-permute-done((bf16[96,256]{1,0:T(8,128)(2,1)S(1)}, bf16[96,256]{1,0:T(8,128)(2,1)S(1)}, u32[]{:S(2)}, u32[]{:S(2)}) %collective-permute-start.1) | collective-permute-done | bytes 49184 | tf_op jit(solution)/shard_map/ppermute | solution.py:35
  10.0 1.8 %collective-permute-done = bf16[96,256]{1,0:T(8,128)(2,1)S(1)} collective-permute-done((bf16[96,256]{1,0:T(8,128)(2,1)S(1)}, bf16[96,256]{1,0:T(8,128)(2,1)S(1)}, u32[]{:S(2)}, u32[]{:S(2)}) %collective-permute-start) | collective-permute-done | bytes 49184 | tf_op jit(solution)/shard_map/ppermute | solution.py:35
  11.9 1.4 %collective-permute-start.2 = (bf16[288,256]{1,0:T(8,128)(2,1)S(1)}, bf16[288,256]{1,0:T(8,128)(2,1)S(1)}, u32[]{:S(2)}, u32[]{:S(2)}) collective-permute-start(bf16[288,256]{1,0:T(8,128)(2,1)S(1)} %get-tuple-element.41), channel_id=1, source_target_pairs={{0,8},{1,5},{2,10},{3,7},{4,12},{5,3},{6,14},{7,1},{8,16},{9,13},{... | collective-permute-start | bytes 442376 | tf_op jit(solution)/shard_map/ppermute | solution.py:35
  13.3 1.2 %collective-permute-start.5 = (bf16[384,256]{1,0:T(8,128)(2,1)S(1)}, bf16[384,256]{1,0:T(8,128)(2,1)S(1)}, u32[]{:S(2)}, u32[]{:S(2)}) collective-permute-start(bf16[384,256]{1,0:T(8,128)(2,1)S(1)} %copy-done), channel_id=1, source_target_pairs={{0,1},{1,0},{2,3},{3,2},{4,5},{5,4},{6,7},{7,6},{8,9},{9,8},{10,11... | collective-permute-start | bytes 589832 | tf_op jit(solution)/shard_map/ppermute | solution.py:35
  14.5 2.7 %collective-permute-start.4 = (bf16[288,256]{1,0:T(8,128)(2,1)S(1)}, bf16[288,256]{1,0:T(8,128)(2,1)S(1)}, u32[]{:S(2)}, u32[]{:S(2)}) collective-permute-start(bf16[288,256]{1,0:T(8,128)(2,1)S(1)} %get-tuple-element.39), channel_id=1, source_target_pairs={{0,24},{1,7},{2,26},{3,5},{4,28},{5,1},{6,30},{7,3},{8,0},{9,15},{... | collective-permute-start | bytes 442376 | tf_op jit(solution)/shard_map/ppermute | solution.py:35
  17.6 5.2 %collective-permute-done.3 = bf16[288,256]{1,0:T(8,128)(2,1)S(1)} collective-permute-done((bf16[288,256]{1,0:T(8,128)(2,1)S(1)}, bf16[288,256]{1,0:T(8,128)(2,1)S(1)}, u32[]{:S(2)}, u32[]{:S(2)}) %collective-permute-start.3) | collective-permute-done | bytes 147488 | tf_op jit(solution)/shard_map/ppermute | solution.py:35
  23.0 1.2 %collective-permute-start.8 = (bf16[768,256]{1,0:T(8,128)(2,1)S(1)}, bf16[768,256]{1,0:T(8,128)(2,1)S(1)}, u32[]{:S(2)}, u32[]{:S(2)}) collective-permute-start(bf16[768,256]{1,0:T(8,128)(2,1)S(1)} %get-tuple-element.31), channel_id=1, source_target_pairs={{0,4},{1,9},{2,6},{3,11},{4,2},{5,13},{6,0},{7,15},{8,12},{9,17},{... | collective-permute-start | bytes 1179656 | tf_op jit(solution)/shard_map/ppermute | solution.py:35
  24.2 1.6 %collective-permute-start.7 = (bf16[768,256]{1,0:T(8,128)(2,1)S(1)}, bf16[768,256]{1,0:T(8,128)(2,1)S(1)}, u32[]{:S(2)}, u32[]{:S(2)}) collective-permute-start(bf16[768,256]{1,0:T(8,128)(2,1)S(1)} %get-tuple-element.32), channel_id=1, source_target_pairs={{0,6},{1,25},{2,4},{3,27},{4,0},{5,29},{6,2},{7,31},{8,14},{9,1},{... | collective-permute-start | bytes 1179656 | tf_op jit(solution)/shard_map/ppermute | solution.py:35
  25.8 2.8 %shard_map.47 = (f32[136,768]{1,0:T(8,128)S(1)}, f32[136,768]{1,0:T(8,128)S(1)}) custom-call(s32[64]{0:T(128)S(1)} %copy-done.3, bf16[384,256]{1,0:T(8,128)(2,1)S(1)} %copy-done, bf16[384,256]{1,0:T(8,128)(2,1)S(1)} %collective-permute-done.5.refs_2_.refs_1_, bf16[1248,256]{1,0:T(8,128)(2,1)S(1)} %constant_dynamic-update-slice_fusion.refs_3_), custom_call_target="tpu_custom_call" | custom-call | flops 981467136 | bytes 393216 | tf_op jit(solution)/shard_map/pallas_call | solution.py:198
  28.6 1.4 %collective-permute-start.6 = (bf16[864,256]{1,0:T(8,128)(2,1)S(1)}, bf16[864,256]{1,0:T(8,128)(2,1)S(1)}, u32[]{:S(2)}, u32[]{:S(2)}) collective-permute-start(bf16[864,256]{1,0:T(8,128)(2,1)S(1)} %constant_dynamic-slice_fusion.2), channel_id=1, source_target_pairs={{0,2},{1,17},{2,0},{3,19},{4,6},{5,21},{6,4},{7,23},{8,10},{9,25},... | collective-permute-start | bytes 1327112 | tf_op jit(solution)/shard_map/ppermute | solution.py:35
  30.0 1.2 %collective-permute-done.8.refs_3_ = bf16[768,256]{1,0:T(8,128)(2,1)S(1)} collective-permute-done((bf16[768,256]{1,0:T(8,128)(2,1)S(1)}, bf16[768,256]{1,0:T(8,128)(2,1)S(1)}, u32[]{:S(2)}, u32[]{:S(2)}) %collective-permute-start.8) | collective-permute-done | bytes 393248 | tf_op jit(solution)/shard_map/ppermute | solution.py:35
  31.2 0.8 %shard_map.48 = (f32[136,768]{1,0:T(8,128)S(1)}, f32[136,768]{1,0:T(8,128)S(1)}) custom-call(s32[64]{0:T(128)S(1)} %copy-done.3, bf16[384,256]{1,0:T(8,128)(2,1)S(1)} %copy-done, bf16[384,256]{1,0:T(8,128)(2,1)S(1)} %collective-permute-done.5.refs_2_.refs_1_, bf16[768,256]{1,0:T(8,128)(2,1)S(1)} %collective-permute-done.8.refs_3_, ...), custom_call_target="tpu_custom_call" | custom-call | flops 603979776 | bytes 393216 | tf_op jit(solution)/shard_map/pallas_call | solution.py:198
  32.0 3.2 %collective-permute-done.7.refs_3_ = bf16[768,256]{1,0:T(8,128)(2,1)S(1)} collective-permute-done((bf16[768,256]{1,0:T(8,128)(2,1)S(1)}, bf16[768,256]{1,0:T(8,128)(2,1)S(1)}, u32[]{:S(2)}, u32[]{:S(2)}) %collective-permute-start.7) | collective-permute-done | bytes 393248 | tf_op jit(solution)/shard_map/ppermute | solution.py:35
  35.2 0.8 %shard_map.49 = (f32[136,768]{1,0:T(8,128)S(1)}, f32[136,768]{1,0:T(8,128)S(1)}) custom-call(s32[64]{0:T(128)S(1)} %copy-done.3, bf16[384,256]{1,0:T(8,128)(2,1)S(1)} %copy-done, bf16[384,256]{1,0:T(8,128)(2,1)S(1)} %collective-permute-done.5.refs_2_.refs_1_, bf16[768,256]{1,0:T(8,128)(2,1)S(1)} %collective-permute-done.7.refs_3_, ...), custom_call_target="tpu_custom_call" | custom-call | flops 603979776 | bytes 393216 | tf_op jit(solution)/shard_map/pallas_call | solution.py:198
  36.1 1.8 %collective-permute-done.6.refs_2_ = bf16[864,256]{1,0:T(8,128)(2,1)S(1)} collective-permute-done((bf16[864,256]{1,0:T(8,128)(2,1)S(1)}, bf16[864,256]{1,0:T(8,128)(2,1)S(1)}, u32[]{:S(2)}, u32[]{:S(2)}) %collective-permute-start.6) | collective-permute-done | bytes 442400 | tf_op jit(solution)/shard_map/ppermute | solution.py:35
  37.8 0.8 %shard_map.51 = f32[136,768]{1,0:T(8,128)S(1)} custom-call(s32[64]{0:T(128)S(1)} %copy-done.3, bf16[384,256]{1,0:T(8,128)(2,1)S(1)} %collective-permute-done.5.refs_2_.refs_1_, bf16[864,256]{1,0:T(8,128)(2,1)S(1)} %collective-permute-done.6.refs_2_, f32[136,768]{1,0:T(8,128)S(1)} %get-tuple-element.30.refs_3_), custom_call_target="tpu_custom_call" | custom-call | flops 339738624 | bytes 393216 | tf_op jit(solution)/shard_map/pallas_call | solution.py:198
  38.6 3.1 %collective-permute-start.9 = (f32[136,768]{1,0:T(8,128)S(1)}, f32[136,768]{1,0:T(8,128)S(1)}, u32[]{:S(2)}, u32[]{:S(2)}) collective-permute-start(f32[136,768]{1,0:T(8,128)S(1)} %shard_map.51), channel_id=1, source_target_pairs={{0,1},{1,0},{2,3},{3,2},{4,5},{5,4},{6,7},{7,6},{8,9},{9,8},{10,11... | collective-permute-start | bytes 1253384 | tf_op jit(solution)/shard_map/ppermute | solution.py:35
  41.7 0.8 %shard_map.50.keep_ref = f32[136,768]{1,0:T(8,128)S(1)} custom-call(s32[64]{0:T(128)S(1)} %copy-done.3, bf16[384,256]{1,0:T(8,128)(2,1)S(1)} %copy-done, bf16[864,256]{1,0:T(8,128)(2,1)S(1)} %collective-permute-done.6.refs_2_, f32[136,768]{1,0:T(8,128)S(1)} %get-tuple-element.29.refs_3_), custom_call_target="tpu_custom_call" | custom-call | flops 339738624 | bytes 393216 | tf_op jit(solution)/shard_map/pallas_call | solution.py:198
  42.5 0.6 %collective-permute-done.9.came_ref = f32[136,768]{1,0:T(8,128)S(1)} collective-permute-done((f32[136,768]{1,0:T(8,128)S(1)}, f32[136,768]{1,0:T(8,128)S(1)}, u32[]{:S(2)}, u32[]{:S(2)}) %collective-permute-start.9) | collective-permute-done | bytes 417824 | tf_op jit(solution)/shard_map/ppermute | solution.py:35
  43.1 0.8 %shard_map.52 = bf16[384,256]{1,0:T(8,128)(2,1)} custom-call(f32[136,768]{1,0:T(8,128)S(1)} %shard_map.50.keep_ref, f32[136,768]{1,0:T(8,128)S(1)} %collective-permute-done.9.came_ref), custom_call_target="tpu_custom_call" | custom-call | tf_op jit(solution)/shard_map/pallas_call | solution.py:253
  (27 shorter events, 0.7 us)
Async XLA Ops:
  0.0 0.7 %copy-start.1 = (bf16[96,128]{1,0:T(8,128)(2,1)S(1)}, bf16[96,128]{1,0:T(8,128)(2,1)}, u32[]{:S(2)}) copy-start(bf16[96,128]{1,0:T(8,128)(2,1)} %k_ref.1) | copy-start | bytes 73732
  0.7 0.7 %copy-start.2 = (bf16[96,128]{1,0:T(8,128)(2,1)S(1)}, bf16[96,128]{1,0:T(8,128)(2,1)}, u32[]{:S(2)}) copy-start(bf16[96,128]{1,0:T(8,128)(2,1)} %v_ref.1) | copy-start | bytes 73732
  1.5 8.5 %collective-permute-start.1 = (bf16[96,256]{1,0:T(8,128)(2,1)S(1)}, bf16[96,256]{1,0:T(8,128)(2,1)S(1)}, u32[]{:S(2)}, u32[]{:S(2)}) collective-permute-start(bf16[96,256]{1,0:T(8,128)(2,1)S(1)} %shard_map.46), channel_id=1, source_target_pairs={{0,64},{1,65},{2,66},{3,67},{4,68},{5,69},{6,70},{7,71},{8,72},{9,... | collective-permute-start | bytes 147464 | tf_op jit(solution)/shard_map/ppermute | solution.py:35
  5.4 6.4 %collective-permute-start = (bf16[96,256]{1,0:T(8,128)(2,1)S(1)}, bf16[96,256]{1,0:T(8,128)(2,1)S(1)}, u32[]{:S(2)}, u32[]{:S(2)}) collective-permute-start(bf16[96,256]{1,0:T(8,128)(2,1)S(1)} %shard_map.46), channel_id=1, source_target_pairs={{0,32},{1,33},{2,34},{3,35},{4,36},{5,37},{6,38},{7,39},{8,40},{9,... | collective-permute-start | bytes 147464 | tf_op jit(solution)/shard_map/ppermute | solution.py:35
  11.8 1.4 %copy-start = (bf16[384,256]{1,0:T(8,128)(2,1)S(1)}, bf16[384,256]{1,0:T(8,128)(2,1)}, u32[]{:S(2)}) copy-start(bf16[384,256]{1,0:T(8,128)(2,1)} %refs_1_.7) | copy-start | bytes 589828
  11.9 5.7 %collective-permute-start.2 = (bf16[288,256]{1,0:T(8,128)(2,1)S(1)}, bf16[288,256]{1,0:T(8,128)(2,1)S(1)}, u32[]{:S(2)}, u32[]{:S(2)}) collective-permute-start(bf16[288,256]{1,0:T(8,128)(2,1)S(1)} %get-tuple-element.41), channel_id=1, source_target_pairs={{0,8},{1,5},{2,10},{3,7},{4,12},{5,3},{6,14},{7,1},{8,16},{9,13},{... | collective-permute-start | bytes 442376 | tf_op jit(solution)/shard_map/ppermute | solution.py:35
  13.3 12.5 %collective-permute-start.5 = (bf16[384,256]{1,0:T(8,128)(2,1)S(1)}, bf16[384,256]{1,0:T(8,128)(2,1)S(1)}, u32[]{:S(2)}, u32[]{:S(2)}) collective-permute-start(bf16[384,256]{1,0:T(8,128)(2,1)S(1)} %copy-done), channel_id=1, source_target_pairs={{0,1},{1,0},{2,3},{3,2},{4,5},{5,4},{6,7},{7,6},{8,9},{9,8},{10,11... | collective-permute-start | bytes 589832 | tf_op jit(solution)/shard_map/ppermute | solution.py:35
  14.5 8.3 %collective-permute-start.4 = (bf16[288,256]{1,0:T(8,128)(2,1)S(1)}, bf16[288,256]{1,0:T(8,128)(2,1)S(1)}, u32[]{:S(2)}, u32[]{:S(2)}) collective-permute-start(bf16[288,256]{1,0:T(8,128)(2,1)S(1)} %get-tuple-element.39), channel_id=1, source_target_pairs={{0,24},{1,7},{2,26},{3,5},{4,28},{5,1},{6,30},{7,3},{8,0},{9,15},{... | collective-permute-start | bytes 442376 | tf_op jit(solution)/shard_map/ppermute | solution.py:35
  17.2 5.6 %collective-permute-start.3 = (bf16[288,256]{1,0:T(8,128)(2,1)S(1)}, bf16[288,256]{1,0:T(8,128)(2,1)S(1)}, u32[]{:S(2)}, u32[]{:S(2)}) collective-permute-start(bf16[288,256]{1,0:T(8,128)(2,1)S(1)} %get-tuple-element.40), channel_id=1, source_target_pairs={{0,16},{1,3},{2,18},{3,1},{4,20},{5,7},{6,22},{7,5},{8,24},{9,11},... | collective-permute-start | bytes 442376 | tf_op jit(solution)/shard_map/ppermute | solution.py:35
  23.0 2.8 %copy-start.3 = (s32[64]{0:T(128)S(1)}, s32[64]{0:T(128)}, u32[]{:S(2)}) copy-start(s32[64]{0:T(128)} %refs_0_.9) | copy-start | bytes 772
  23.0 8.2 %collective-permute-start.8 = (bf16[768,256]{1,0:T(8,128)(2,1)S(1)}, bf16[768,256]{1,0:T(8,128)(2,1)S(1)}, u32[]{:S(2)}, u32[]{:S(2)}) collective-permute-start(bf16[768,256]{1,0:T(8,128)(2,1)S(1)} %get-tuple-element.31), channel_id=1, source_target_pairs={{0,4},{1,9},{2,6},{3,11},{4,2},{5,13},{6,0},{7,15},{8,12},{9,17},{... | collective-permute-start | bytes 1179656 | tf_op jit(solution)/shard_map/ppermute | solution.py:35
  24.2 11.0 %collective-permute-start.7 = (bf16[768,256]{1,0:T(8,128)(2,1)S(1)}, bf16[768,256]{1,0:T(8,128)(2,1)S(1)}, u32[]{:S(2)}, u32[]{:S(2)}) collective-permute-start(bf16[768,256]{1,0:T(8,128)(2,1)S(1)} %get-tuple-element.32), channel_id=1, source_target_pairs={{0,6},{1,25},{2,4},{3,27},{4,0},{5,29},{6,2},{7,31},{8,14},{9,1},{... | collective-permute-start | bytes 1179656 | tf_op jit(solution)/shard_map/ppermute | solution.py:35
  28.6 9.2 %collective-permute-start.6 = (bf16[864,256]{1,0:T(8,128)(2,1)S(1)}, bf16[864,256]{1,0:T(8,128)(2,1)S(1)}, u32[]{:S(2)}, u32[]{:S(2)}) collective-permute-start(bf16[864,256]{1,0:T(8,128)(2,1)S(1)} %constant_dynamic-slice_fusion.2), channel_id=1, source_target_pairs={{0,2},{1,17},{2,0},{3,19},{4,6},{5,21},{6,4},{7,23},{8,10},{9,25},... | collective-permute-start | bytes 1327112 | tf_op jit(solution)/shard_map/ppermute | solution.py:35
  38.6 4.5 %collective-permute-start.9 = (f32[136,768]{1,0:T(8,128)S(1)}, f32[136,768]{1,0:T(8,128)S(1)}, u32[]{:S(2)}, u32[]{:S(2)}) collective-permute-start(f32[136,768]{1,0:T(8,128)S(1)} %shard_map.51), channel_id=1, source_target_pairs={{0,1},{1,0},{2,3},{3,2},{4,5},{5,4},{6,7},{7,6},{8,9},{9,8},{10,11... | collective-permute-start | bytes 1253384 | tf_op jit(solution)/shard_map/ppermute | solution.py:35

commit v2 on v1

--- a/solution.py
+++ b/solution.py
@@ -16,6 +16,8 @@
 
 WIDE = 8
 LAST = 8
+
+X_FIRST = 1
 
 
 def device_index(pair, y, core):
@@ -44,11 +46,11 @@
 
 
 def first_axis(by):
-    return lambda pair, y, core: (along_x(pair, by), y, core) if core == 0 else (pair, y + by, core)
+    return lambda pair, y, core: (along_x(pair, by), y, core) if core == X_FIRST else (pair, y + by, core)
 
 
 def second_axis(by):
-    return lambda pair, y, core: (pair, y + by, core) if core == 0 else (along_x(pair, by), y, core)
+    return lambda pair, y, core: (pair, y + by, core) if core == X_FIRST else (along_x(pair, by), y, core)
 
 
 def other_core(pair, y, core):
@@ -69,26 +71,22 @@
 
 
 def near_starts(core, start_of):
-    return [jnp.where(core == 0, start_of(i, 0), start_of(i // NY * NX, i % NY)) for i in range(WIDE)]
+    return [jnp.where(core == X_FIRST, start_of(i, 0), start_of(i // NY * NX, i % NY)) for i in range(WIDE)]
 
 
 def far_starts(core, start_of):
-    return [start_of(LAST, 0)] + [jnp.where(core == 0, FAR, start_of(LAST, turn)) for turn in (1, 2, 3)]
+    return [start_of(LAST, 0)] + [jnp.where(core == X_FIRST, FAR, start_of(LAST, turn)) for turn in (1, 2, 3)]
 
 
 def side_starts(core, y, start_of, by):
     skip = (y + by) % 2 if by != 2 else 0
     return [
-        jnp.where(core == 0, start_of(i + skip, by), start_of(i // NY * NX + by, i % NY)) for i in range(WIDE)
+        jnp.where(core == X_FIRST, start_of(i + skip, by), start_of(i // NY * NX + by, i % NY)) for i in range(WIDE)
     ]
 
 
-def last_starts(core, start_of):
-    return [jnp.where(core == 0, start_of(LAST, 2), FAR)]
-
-
 def attend_kernel(names, groups, chunk, scale, opening, *refs):
-    lens = refs[0]
+    docs = refs[0]
     q_refs = refs[1 : 1 + groups]
     kv = dict(zip(names, refs[1 + groups :]))
     refs = refs[1 + groups + len(names) :]
@@ -96,7 +94,7 @@
     head_dim = kv[names[0]].shape[1] // 2
     heads_here = q_refs[0].shape[1] // head_dim
     row_m, row_l = slice(head_dim, head_dim + 1), slice(head_dim + 1, head_dim + 2)
-    state = refs if opening else refs[groups:]
+    state = refs[:groups] if opening else refs[groups:]
     for group, ref in enumerate(state):
         if opening:
             ref[...] = jnp.zeros(ref.shape, jnp.float32)
@@ -108,14 +106,16 @@
     first_row = ctx * rows
     last_row = first_row + (rows - 1)
     q_pos = first_row + lax.broadcasted_iota(jnp.int32, (1, rows), 1)
-    end = jnp.int32(0)
-    first_doc = last_doc = jnp.int32(0)
-    doc_start = jnp.zeros((1, rows), jnp.int32)
-    for i in range(lens.shape[0]):
-        end = end + lens[i]
-        doc_start = jnp.where(end <= q_pos, end, doc_start)
-        first_doc = jnp.where(end <= first_row, end, first_doc)
-        last_doc = jnp.where(end <= last_row, end, last_doc)
+    if opening:
+        end = jnp.int32(0)
+        doc_start = jnp.zeros((1, rows), jnp.int32)
+        for i in range(docs.shape[0]):
+            end = end + docs[i]
+            doc_start = jnp.where(end <= q_pos, end, doc_start)
+        refs[groups][...] = doc_start
+    else:
+        doc_start = docs[...]
+    first_doc, last_doc = jnp.min(doc_start), jnp.max(doc_start)
 
     def absorb(tile, starts, masked):
         keys = len(starts) * chunk
@@ -161,52 +161,77 @@
             waiting = (group, h, p, alpha)
         finish(*waiting)
 
-    def absorb_if_needed(load, starts):
+    def reach_of(starts):
         needed = full = None
         for start in starts:
             here = (start + (chunk - 1) >= first_doc) & (start <= last_row)
             whole = (start >= last_doc) & (start + (chunk - 1) <= first_row)
             needed = here if needed is None else needed | here
             full = whole if full is None else full & whole
+        return needed, full
+
+    def absorb_if_needed(ref, begin, starts, halves=False):
+        near, far = starts[: len(starts) // 2], starts[len(starts) // 2 :]
+        needed, full = reach_of(starts)
+
+        def part(count):
+            return ref[begin * chunk : (begin + count) * chunk, :]
 
         @pl.when(full)
         def _():
-            absorb(load(), starts, False)
+            absorb(part(len(starts)), starts, False)
+
+        if halves:
+            beyond, _ = reach_of(far)
+
+            @pl.when(needed & jnp.logical_not(beyond))
+            def _():
+                absorb(part(len(near)), near, True)
+
+            needed = beyond
 
         @pl.when(needed & jnp.logical_not(full))
         def _():
-            absorb(load(), starts, True)
-
-    wide = WIDE * chunk
+            absorb(part(len(starts)), starts, True)
+
     if "own" in kv:
-        absorb_if_needed(lambda: kv["own"][:wide, :], near_starts(core, start_of))
-        absorb_if_needed(lambda: kv["own"][wide : wide + NY * chunk, :], far_starts(core, start_of))
-    for by in (1, 3, 2):
-        if by in kv:
-            absorb_if_needed(lambda by=by: kv[by][:wide, :], side_starts(core, y, start_of, by))
+        absorb_if_needed(kv["own"], 0, near_starts(core, start_of), True)
+        absorb_if_needed(kv["own"], WIDE, far_starts(core, start_of))
+    half = WIDE // 2
     if 2 in kv:
-        absorb_if_needed(lambda: kv[2][wide:, :], last_starts(core, start_of))
-
-
-def attend(lens, qs, kv, states, chunk, head_dim, scale):
+        two = side_starts(core, y, start_of, 2)
+        absorb_if_needed(kv[2], 0, two, True)
+        absorb_if_needed(kv[2], WIDE, [jnp.where(core == X_FIRST, start_of(LAST, 2), FAR)])
+    for by in (1, 3):
+        starts = side_starts(core, y, start_of, by)
+        if (by, 0) in kv:
+            absorb_if_needed(kv[by, 0], 0, starts[:half])
+        if (by, 1) in kv:
+            absorb_if_needed(kv[by, 1], 0, starts[half:])
+
+
+def attend(docs, qs, kv, states, chunk, head_dim, scale):
     smem = pl.BlockSpec(memory_space=pltpu.SMEM)
     vmem = pl.BlockSpec(memory_space=pltpu.VMEM)
     rows = qs[0].shape[0] * (qs[0].shape[1] // head_dim)
     names, arrays = tuple(kv), list(kv.values())
     keys = sum(array.shape[0] for array in arrays)
     given = list(states or [])
+    out = [jax.ShapeDtypeStruct((head_dim + 8, rows), jnp.float32)] * len(qs)
+    if states is None:
+        out += [jax.ShapeDtypeStruct((1, qs[0].shape[0]), jnp.int32)]
     return pl.pallas_call(
         functools.partial(attend_kernel, names, len(qs), chunk, scale, states is None),
-        out_shape=[jax.ShapeDtypeStruct((head_dim + 8, rows), jnp.float32)] * len(qs),
-        in_specs=[smem] + [vmem] * (len(qs) + len(arrays) + len(given)),
-        out_specs=[vmem] * len(qs),
+        out_shape=out,
+        in_specs=[smem if states is None else vmem] + [vmem] * (len(qs) + len(arrays) + len(given)),
+        out_specs=[vmem] * len(out),
         compiler_params=pltpu.CompilerParams(vmem_limit_bytes=32 * 1024 * 1024),
         cost_estimate=pl.CostEstimate(
             flops=4 * keys * rows * len(qs) * head_dim,
             bytes_accessed=4 * rows * head_dim,
             transcendentals=keys * rows * len(qs),
         ),
-    )(lens, *qs, *arrays, *given)
+    )(docs, *qs, *arrays, *given)
 
 
 def join_kernel(k_ref, v_ref, out_ref, sems):
@@ -269,39 +294,46 @@
     own = join(key_rows, value_rows)
     back8 = send(own, later_plane(2))
     back4 = send(own, later_plane(1))
-    own, back4, back8, late_q = lax.optimization_barrier((own, back4, back8, queries))
+    back4, back8, late_q = lax.optimization_barrier((back4, back8, queries))
     other_q = send(late_q, other_core)
 
     def round_x(by):
         return (ctx // 2) % NX + by >= NX
 
     def first(by):
-        wraps = (core == 0) & round_x(by)
+        wraps = (core == X_FIRST) & round_x(by)
         parts = [jnp.where(wraps, back4, own), jnp.where(wraps, back8, back4), back8]
         return send(jnp.concatenate(parts, axis=0), first_axis(by))
 
-    got = {by: first(by) for by in (1, 3, 2)}
+    got = {by: first(by) for by in (2, 1, 3)}
     planes = [own, back4, back8]
     held = []
     for i, plane in enumerate(planes):
         held += [plane] + [got[by][i * chunk : (i + 1) * chunk] for by in (1, 2, 3)]
     held = jnp.concatenate(held + [own], axis=0)
 
-    def second(by, chunks):
-        begin = jnp.where(core == 0, ctx % 2 if by != 2 else 0, jnp.where(round_x(by), NY, 0))
+    def second(by, first, chunks):
+        begin = jnp.where(core == X_FIRST, ctx % 2 if by != 2 else 0, jnp.where(round_x(by), NY, 0)) + first
         return send(lax.dynamic_slice_in_dim(held, begin * chunk, chunks * chunk, 0), second_axis(by))
 
-    b1, b3 = second(1, WIDE), second(3, WIDE)
-    call = functools.partial(attend, doc_lengths, chunk=chunk, head_dim=head_dim, scale=scale)
+    half = WIDE // 2
+    sides = {2: second(2, 0, WIDE + 1)}
+    for part in (0, 1):
+        for by in (1, 3):
+            sides[by, part] = second(by, part * half, half)
+    call = functools.partial(attend, chunk=chunk, head_dim=head_dim, scale=scale)
     both = [queries, other_q]
-    states = call(both, {"own": held}, None)
-    held, *states = lax.optimization_barrier((held, *states))
-    b2 = second(2, WIDE + 1)
-    states = call(both, {1: b1}, states)
-    keep, away = call(both, {3: b3}, states)
-    (away,) = call([other_q], {2: b2}, [away])
+    *states, docs = call(doc_lengths, both, {"own": held}, None)
+
+    def some(*keys):
+        return {key: sides[key] for key in keys}
+
+    states = call(docs, both, some(2), states)
+    keep, away = call(docs, both, some((1, 0), (3, 0)), states)
+    last = some((1, 1), (3, 1))
+    (away,) = call(docs, [other_q], last, [away])
     came = send(away, other_core)
-    (keep,) = call([queries], {2: b2}, [keep])
+    (keep,) = call(docs, [queries], last, [keep])
     return merge(keep, came, row_count, head_dim, scale)
 
 

time: 44.1 us -> 41.1 us (0.932)
  waiting for transfers between devices: 16.8 us -> 8.49 us
  starting transfers between devices: 18.4 us -> 24.8 us
  Pallas kernels: 6.83 us -> 5.44 us
    ppermute x10 -> x12, waiting for transfers between devices: 16.8 us -> 8.49 us  [send(): return lax.ppermute(array, ('ctx', 'head'), sorted(pairs))]
    ppermute x10 -> x12, starting transfers between devices: 18.4 us -> 24.8 us  [send(): return lax.ppermute(array, ('ctx', 'head'), sorted(pairs))]
    pallas_call x5, Pallas kernels: 5.96 us -> 4.58 us  [attend(): pl.pallas_call(functools.partial(attend_kernel, names, len(qs), chunk, sc...]
  transfers between devices with their start and end apart: 10 -> 12, of which waited for: 7 -> 6; matrix products, arithmetic and copies ran while one was open for 0% -> 0% of each run, Pallas kernels for 12% -> 11%
where the time goes in v2:
time: 41.1 us; the launch traced here: 40.6 us
  starting transfers between devices  24.8 us (60%)
  waiting for transfers between devices  8.49 us (21%)
  Pallas kernels  5.44 us (13%)
  local copies, waits for them, and re-layouts  1.64 us (4%)
    ppermute x12, starting transfers between devices, send(): return lax.ppermute(array, ('ctx', 'head'), sorted(pairs))  24.8 us
    ppermute x12, waiting for transfers between devices, send(): return lax.ppermute(array, ('ctx', 'head'), sorted(pairs))  8.49 us
    pallas_call x5, Pallas kernels, attend(): pl.pallas_call(functools.partial(attend_kernel, names, len(qs), chunk, sc...  4.58 us
    unnamed x19, local copies, waits for them, and re-layouts  1.54 us
    pallas_call x1, Pallas kernels, merge(): pl.pallas_call(functools.partial(merge_kernel, head_dim, scale), out_shap...  0.84 us
  transfers between devices with their start and end apart: 12, of which 6 were waited for; matrix products, arithmetic and copies ran while one was open for 0% of the time, Pallas kernels for 11%

profile of v2, /device:TPU:1, one launch (start us, length us, event | category | flops | bytes accessed | tf_op | source)
XLA Modules:
  0.0 40.6 jit_solution(12611591281877404737)
XLA Ops:
  0.0 0.7 %copy-done.1 = bf16[96,128]{1,0:T(8,128)(2,1)S(1)} copy-done((bf16[96,128]{1,0:T(8,128)(2,1)S(1)}, bf16[96,128]{1,0:T(8,128)(2,1)}, u32[]{:S(2)}) %copy-start.1) | copy-done | bytes 24600
  0.7 0.7 %copy-done.2 = bf16[96,128]{1,0:T(8,128)(2,1)S(1)} copy-done((bf16[96,128]{1,0:T(8,128)(2,1)S(1)}, bf16[96,128]{1,0:T(8,128)(2,1)}, u32[]{:S(2)}) %copy-start.2) | copy-done | bytes 24600
  1.5 2.5 %collective-permute-start = (bf16[96,256]{1,0:T(8,128)(2,1)S(1)}, bf16[96,256]{1,0:T(8,128)(2,1)S(1)}, u32[]{:S(2)}, u32[]{:S(2)}) collective-permute-start(bf16[96,256]{1,0:T(8,128)(2,1)S(1)} %shard_map.46), channel_id=1, source_target_pairs={{0,32},{1,33},{2,34},{3,35},{4,36},{5,37},{6,38},{7,39},{8,40},{9,... | collective-permute-start | bytes 147464 | tf_op jit(solution)/shard_map/ppermute | solution.py:37
  4.1 3.0 %collective-permute-start.1 = (bf16[96,256]{1,0:T(8,128)(2,1)S(1)}, bf16[96,256]{1,0:T(8,128)(2,1)S(1)}, u32[]{:S(2)}, u32[]{:S(2)}) collective-permute-start(bf16[96,256]{1,0:T(8,128)(2,1)S(1)} %shard_map.46), channel_id=1, source_target_pairs={{0,64},{1,65},{2,66},{3,67},{4,68},{5,69},{6,70},{7,71},{8,72},{9,... | collective-permute-start | bytes 147464 | tf_op jit(solution)/shard_map/ppermute | solution.py:37
  7.1 2.4 %collective-permute-done = bf16[96,256]{1,0:T(8,128)(2,1)S(1)} collective-permute-done((bf16[96,256]{1,0:T(8,128)(2,1)S(1)}, bf16[96,256]{1,0:T(8,128)(2,1)S(1)}, u32[]{:S(2)}, u32[]{:S(2)}) %collective-permute-start) | collective-permute-done | bytes 49184 | tf_op jit(solution)/shard_map/ppermute | solution.py:37
  9.5 1.8 %collective-permute-done.1 = bf16[96,256]{1,0:T(8,128)(2,1)S(1)} collective-permute-done((bf16[96,256]{1,0:T(8,128)(2,1)S(1)}, bf16[96,256]{1,0:T(8,128)(2,1)S(1)}, u32[]{:S(2)}, u32[]{:S(2)}) %collective-permute-start.1) | collective-permute-done | bytes 49184 | tf_op jit(solution)/shard_map/ppermute | solution.py:37
  11.4 1.3 %collective-permute-start.3 = (bf16[288,256]{1,0:T(8,128)(2,1)S(1)}, bf16[288,256]{1,0:T(8,128)(2,1)S(1)}, u32[]{:S(2)}, u32[]{:S(2)}) collective-permute-start(bf16[288,256]{1,0:T(8,128)(2,1)S(1)} %get-tuple-element.37), channel_id=1, source_target_pairs={{0,4},{1,9},{2,6},{3,11},{4,2},{5,13},{6,0},{7,15},{8,12},{9,17},{... | collective-permute-start | bytes 442376 | tf_op jit(solution)/shard_map/ppermute | solution.py:37
  12.7 2.5 %collective-permute-start.4 = (bf16[288,256]{1,0:T(8,128)(2,1)S(1)}, bf16[288,256]{1,0:T(8,128)(2,1)S(1)}, u32[]{:S(2)}, u32[]{:S(2)}) collective-permute-start(bf16[288,256]{1,0:T(8,128)(2,1)S(1)} %get-tuple-element.36), channel_id=1, source_target_pairs={{0,2},{1,17},{2,0},{3,19},{4,6},{5,21},{6,4},{7,23},{8,10},{9,25},... | collective-permute-start | bytes 442376 | tf_op jit(solution)/shard_map/ppermute | solution.py:37
  15.1 1.2 %collective-permute-start.5 = (bf16[288,256]{1,0:T(8,128)(2,1)S(1)}, bf16[288,256]{1,0:T(8,128)(2,1)S(1)}, u32[]{:S(2)}, u32[]{:S(2)}) collective-permute-start(bf16[288,256]{1,0:T(8,128)(2,1)S(1)} %get-tuple-element.35), channel_id=1, source_target_pairs={{0,6},{1,25},{2,4},{3,27},{4,0},{5,29},{6,2},{7,31},{8,14},{9,1},{... | collective-permute-start | bytes 442376 | tf_op jit(solution)/shard_map/ppermute | solution.py:37
  16.3 0.4 collective-permute-done.3
  16.7 2.6 %collective-permute-done.4 = bf16[288,256]{1,0:T(8,128)(2,1)S(1)} collective-permute-done((bf16[288,256]{1,0:T(8,128)(2,1)S(1)}, bf16[288,256]{1,0:T(8,128)(2,1)S(1)}, u32[]{:S(2)}, u32[]{:S(2)}) %collective-permute-start.4) | collective-permute-done | bytes 147488 | tf_op jit(solution)/shard_map/ppermute | solution.py:37
  19.6 2.8 %collective-permute-start.10 = (bf16[864,256]{1,0:T(8,128)(2,1)S(1)}, bf16[864,256]{1,0:T(8,128)(2,1)S(1)}, u32[]{:S(2)}, u32[]{:S(2)}) collective-permute-start(bf16[864,256]{1,0:T(8,128)(2,1)S(1)} %constant_dynamic-slice_fusion), channel_id=1, source_target_pairs={{0,16},{1,3},{2,18},{3,1},{4,20},{5,7},{6,22},{7,5},{8,24},{9,11},... | collective-permute-start | bytes 1327112 | tf_op jit(solution)/shard_map/ppermute | solution.py:37
  22.4 4.6 %collective-permute-start.2 = (bf16[384,256]{1,0:T(8,128)(2,1)S(1)}, bf16[384,256]{1,0:T(8,128)(2,1)S(1)}, u32[]{:S(2)}, u32[]{:S(2)}) collective-permute-start(bf16[384,256]{1,0:T(8,128)(2,1)S(1)} %copy-done), channel_id=1, source_target_pairs={{0,1},{1,0},{2,3},{3,2},{4,5},{5,4},{6,7},{7,6},{8,9},{9,8},{10,11... | collective-permute-start | bytes 589832 | tf_op jit(solution)/shard_map/ppermute | solution.py:37
  27.0 1.0 %collective-permute-start.8 = (bf16[384,256]{1,0:T(8,128)(2,1)S(1)}, bf16[384,256]{1,0:T(8,128)(2,1)S(1)}, u32[]{:S(2)}, u32[]{:S(2)}) collective-permute-start(bf16[384,256]{1,0:T(8,128)(2,1)S(1)} %get-tuple-element.26), channel_id=1, source_target_pairs={{0,8},{1,5},{2,10},{3,7},{4,12},{5,3},{6,14},{7,1},{8,16},{9,13},{... | collective-permute-start | bytes 589832 | tf_op jit(solution)/shard_map/ppermute | solution.py:37
  28.0 1.8 %collective-permute-start.9 = (bf16[384,256]{1,0:T(8,128)(2,1)S(1)}, bf16[384,256]{1,0:T(8,128)(2,1)S(1)}, u32[]{:S(2)}, u32[]{:S(2)}) collective-permute-start(bf16[384,256]{1,0:T(8,128)(2,1)S(1)} %get-tuple-element.25), channel_id=1, source_target_pairs={{0,24},{1,7},{2,26},{3,5},{4,28},{5,1},{6,30},{7,3},{8,0},{9,15},{... | collective-permute-start | bytes 589832 | tf_op jit(solution)/shard_map/ppermute | solution.py:37
  29.8 2.7 %collective-permute-start.7 = (bf16[384,256]{1,0:T(8,128)(2,1)S(1)}, bf16[384,256]{1,0:T(8,128)(2,1)S(1)}, u32[]{:S(2)}, u32[]{:S(2)}) collective-permute-start(bf16[384,256]{1,0:T(8,128)(2,1)S(1)} %get-tuple-element.27), channel_id=1, source_target_pairs={{0,24},{1,7},{2,26},{3,5},{4,28},{5,1},{6,30},{7,3},{8,0},{9,15},{... | collective-permute-start | bytes 589832 | tf_op jit(solution)/shard_map/ppermute | solution.py:37
  32.5 2.2 %shard_map.47 = (f32[136,768]{1,0:T(8,128)S(1)}, f32[136,768]{1,0:T(8,128)S(1)}, s32[1,384]{1,0:T(1,128)S(1)}) custom-call(s32[64]{0:T(128)S(1)} %copy-done.3, bf16[384,256]{1,0:T(8,128)(2,1)S(1)} %copy-done, bf16[384,256]{1,0:T(8,128)(2,1)S(1)} %collective-permute-done.2.refs_2_.refs_1_, bf16[1248,256]{1,0:T(8,128)(2,1)S(1)} %constant_dynamic-update-slice_fusion.refs_3_), custom_call_target="tpu_custom_call" | custom-call | flops 981467136 | bytes 393216 | tf_op jit(solution)/shard_map/pallas_call | solution.py:223
  34.7 1.4 %shard_map.48 = (f32[136,768]{1,0:T(8,128)S(1)}, f32[136,768]{1,0:T(8,128)S(1)}) custom-call(s32[1,384]{1,0:T(1,128)S(1)} %get-tuple-element.18.refs_0_, bf16[384,256]{1,0:T(8,128)(2,1)S(1)} %copy-done, bf16[384,256]{1,0:T(8,128)(2,1)S(1)} %collective-permute-done.2.refs_2_.refs_1_, bf16[864,256]{1,0:T(8,128)(2,1)S(1)} %collective-permute-done.10.refs_3_, ...), custom_call_target="tpu_custom_call" | custom-call | flops 679477248 | bytes 393216 | tf_op jit(solution)/shard_map/pallas_call | solution.py:223
  36.1 0.5 %shard_map.49 = (f32[136,768]{1,0:T(8,128)S(1)}, f32[136,768]{1,0:T(8,128)S(1)}) custom-call(s32[1,384]{1,0:T(1,128)S(1)} %get-tuple-element.18.refs_0_, bf16[384,256]{1,0:T(8,128)(2,1)S(1)} %copy-done, bf16[384,256]{1,0:T(8,128)(2,1)S(1)} %collective-permute-done.2.refs_2_.refs_1_, bf16[384,256]{1,0:T(8,128)(2,1)S(1)} %collective-permute-done.8.refs_3_, ...), custom_call_target="tpu_custom_call" | custom-call | flops 603979776 | bytes 393216 | tf_op jit(solution)/shard_map/pallas_call | solution.py:223
  36.6 0.3 shard_map.51
  36.9 1.5 %collective-permute-start.11 = (f32[136,768]{1,0:T(8,128)S(1)}, f32[136,768]{1,0:T(8,128)S(1)}, u32[]{:S(2)}, u32[]{:S(2)}) collective-permute-start(f32[136,768]{1,0:T(8,128)S(1)} %shard_map.51), channel_id=1, source_target_pairs={{0,1},{1,0},{2,3},{3,2},{4,5},{5,4},{6,7},{7,6},{8,9},{9,8},{10,11... | collective-permute-start | bytes 1253384 | tf_op jit(solution)/shard_map/ppermute | solution.py:37
  38.4 0.3 shard_map.50.keep_ref
  38.7 1.1 %collective-permute-done.11.came_ref = f32[136,768]{1,0:T(8,128)S(1)} collective-permute-done((f32[136,768]{1,0:T(8,128)S(1)}, f32[136,768]{1,0:T(8,128)S(1)}, u32[]{:S(2)}, u32[]{:S(2)}) %collective-permute-start.11) | collective-permute-done | bytes 417824 | tf_op jit(solution)/shard_map/ppermute | solution.py:37
  39.8 0.8 %shard_map.52 = bf16[384,256]{1,0:T(8,128)(2,1)} custom-call(f32[136,768]{1,0:T(8,128)S(1)} %shard_map.50.keep_ref, f32[136,768]{1,0:T(8,128)S(1)} %collective-permute-done.11.came_ref), custom_call_target="tpu_custom_call" | custom-call | tf_op jit(solution)/shard_map/pallas_call | solution.py:278
  (31 shorter events, 0.5 us)
Async XLA Ops:
  0.0 0.7 %copy-start.1 = (bf16[96,128]{1,0:T(8,128)(2,1)S(1)}, bf16[96,128]{1,0:T(8,128)(2,1)}, u32[]{:S(2)}) copy-start(bf16[96,128]{1,0:T(8,128)(2,1)} %k_ref.1) | copy-start | bytes 73732
  0.7 0.7 %copy-start.2 = (bf16[96,128]{1,0:T(8,128)(2,1)S(1)}, bf16[96,128]{1,0:T(8,128)(2,1)}, u32[]{:S(2)}) copy-start(bf16[96,128]{1,0:T(8,128)(2,1)} %v_ref.1) | copy-start | bytes 73732
  1.5 8.0 %collective-permute-start = (bf16[96,256]{1,0:T(8,128)(2,1)S(1)}, bf16[96,256]{1,0:T(8,128)(2,1)S(1)}, u32[]{:S(2)}, u32[]{:S(2)}) collective-permute-start(bf16[96,256]{1,0:T(8,128)(2,1)S(1)} %shard_map.46), channel_id=1, source_target_pairs={{0,32},{1,33},{2,34},{3,35},{4,36},{5,37},{6,38},{7,39},{8,40},{9,... | collective-permute-start | bytes 147464 | tf_op jit(solution)/shard_map/ppermute | solution.py:37
  4.1 7.2 %collective-permute-start.1 = (bf16[96,256]{1,0:T(8,128)(2,1)S(1)}, bf16[96,256]{1,0:T(8,128)(2,1)S(1)}, u32[]{:S(2)}, u32[]{:S(2)}) collective-permute-start(bf16[96,256]{1,0:T(8,128)(2,1)S(1)} %shard_map.46), channel_id=1, source_target_pairs={{0,64},{1,65},{2,66},{3,67},{4,68},{5,69},{6,70},{7,71},{8,72},{9,... | collective-permute-start | bytes 147464 | tf_op jit(solution)/shard_map/ppermute | solution.py:37
  11.4 5.3 %collective-permute-start.3 = (bf16[288,256]{1,0:T(8,128)(2,1)S(1)}, bf16[288,256]{1,0:T(8,128)(2,1)S(1)}, u32[]{:S(2)}, u32[]{:S(2)}) collective-permute-start(bf16[288,256]{1,0:T(8,128)(2,1)S(1)} %get-tuple-element.37), channel_id=1, source_target_pairs={{0,4},{1,9},{2,6},{3,11},{4,2},{5,13},{6,0},{7,15},{8,12},{9,17},{... | collective-permute-start | bytes 442376 | tf_op jit(solution)/shard_map/ppermute | solution.py:37
  12.7 6.6 %collective-permute-start.4 = (bf16[288,256]{1,0:T(8,128)(2,1)S(1)}, bf16[288,256]{1,0:T(8,128)(2,1)S(1)}, u32[]{:S(2)}, u32[]{:S(2)}) collective-permute-start(bf16[288,256]{1,0:T(8,128)(2,1)S(1)} %get-tuple-element.36), channel_id=1, source_target_pairs={{0,2},{1,17},{2,0},{3,19},{4,6},{5,21},{6,4},{7,23},{8,10},{9,25},... | collective-permute-start | bytes 442376 | tf_op jit(solution)/shard_map/ppermute | solution.py:37
  15.1 4.3 %collective-permute-start.5 = (bf16[288,256]{1,0:T(8,128)(2,1)S(1)}, bf16[288,256]{1,0:T(8,128)(2,1)S(1)}, u32[]{:S(2)}, u32[]{:S(2)}) collective-permute-start(bf16[288,256]{1,0:T(8,128)(2,1)S(1)} %get-tuple-element.35), channel_id=1, source_target_pairs={{0,6},{1,25},{2,4},{3,27},{4,0},{5,29},{6,2},{7,31},{8,14},{9,1},{... | collective-permute-start | bytes 442376 | tf_op jit(solution)/shard_map/ppermute | solution.py:37
  19.5 2.9 %copy-start = (bf16[384,256]{1,0:T(8,128)(2,1)S(1)}, bf16[384,256]{1,0:T(8,128)(2,1)}, u32[]{:S(2)}) copy-start(bf16[384,256]{1,0:T(8,128)(2,1)} %refs_1_.7) | copy-start | bytes 589828
  19.6 15.1 %collective-permute-start.10 = (bf16[864,256]{1,0:T(8,128)(2,1)S(1)}, bf16[864,256]{1,0:T(8,128)(2,1)S(1)}, u32[]{:S(2)}, u32[]{:S(2)}) collective-permute-start(bf16[864,256]{1,0:T(8,128)(2,1)S(1)} %constant_dynamic-slice_fusion), channel_id=1, source_target_pairs={{0,16},{1,3},{2,18},{3,1},{4,20},{5,7},{6,22},{7,5},{8,24},{9,11},... | collective-permute-start | bytes 1327112 | tf_op jit(solution)/shard_map/ppermute | solution.py:37
  22.4 7.4 %collective-permute-start.2 = (bf16[384,256]{1,0:T(8,128)(2,1)S(1)}, bf16[384,256]{1,0:T(8,128)(2,1)S(1)}, u32[]{:S(2)}, u32[]{:S(2)}) collective-permute-start(bf16[384,256]{1,0:T(8,128)(2,1)S(1)} %copy-done), channel_id=1, source_target_pairs={{0,1},{1,0},{2,3},{3,2},{4,5},{5,4},{6,7},{7,6},{8,9},{9,8},{10,11... | collective-permute-start | bytes 589832 | tf_op jit(solution)/shard_map/ppermute | solution.py:37
  27.0 9.0 %collective-permute-start.8 = (bf16[384,256]{1,0:T(8,128)(2,1)S(1)}, bf16[384,256]{1,0:T(8,128)(2,1)S(1)}, u32[]{:S(2)}, u32[]{:S(2)}) collective-permute-start(bf16[384,256]{1,0:T(8,128)(2,1)S(1)} %get-tuple-element.26), channel_id=1, source_target_pairs={{0,8},{1,5},{2,10},{3,7},{4,12},{5,3},{6,14},{7,1},{8,16},{9,13},{... | collective-permute-start | bytes 589832 | tf_op jit(solution)/shard_map/ppermute | solution.py:37
  28.0 8.1 %collective-permute-start.9 = (bf16[384,256]{1,0:T(8,128)(2,1)S(1)}, bf16[384,256]{1,0:T(8,128)(2,1)S(1)}, u32[]{:S(2)}, u32[]{:S(2)}) collective-permute-start(bf16[384,256]{1,0:T(8,128)(2,1)S(1)} %get-tuple-element.25), channel_id=1, source_target_pairs={{0,24},{1,7},{2,26},{3,5},{4,28},{5,1},{6,30},{7,3},{8,0},{9,15},{... | collective-permute-start | bytes 589832 | tf_op jit(solution)/shard_map/ppermute | solution.py:37
  29.8 2.7 %copy-start.3 = (s32[64]{0:T(128)S(1)}, s32[64]{0:T(128)}, u32[]{:S(2)}) copy-start(s32[64]{0:T(128)} %refs_0_.1) | copy-start | bytes 772
  29.8 6.8 %collective-permute-start.6 = (bf16[384,256]{1,0:T(8,128)(2,1)S(1)}, bf16[384,256]{1,0:T(8,128)(2,1)S(1)}, u32[]{:S(2)}, u32[]{:S(2)}) collective-permute-start(bf16[384,256]{1,0:T(8,128)(2,1)S(1)} %get-tuple-element.28), channel_id=1, source_target_pairs={{0,8},{1,5},{2,10},{3,7},{4,12},{5,3},{6,14},{7,1},{8,16},{9,13},{... | collective-permute-start | bytes 589832 | tf_op jit(solution)/shard_map/ppermute | solution.py:37
  29.8 6.8 %collective-permute-start.7 = (bf16[384,256]{1,0:T(8,128)(2,1)S(1)}, bf16[384,256]{1,0:T(8,128)(2,1)S(1)}, u32[]{:S(2)}, u32[]{:S(2)}) collective-permute-start(bf16[384,256]{1,0:T(8,128)(2,1)S(1)} %get-tuple-element.27), channel_id=1, source_target_pairs={{0,24},{1,7},{2,26},{3,5},{4,28},{5,1},{6,30},{7,3},{8,0},{9,15},{... | collective-permute-start | bytes 589832 | tf_op jit(solution)/shard_map/ppermute | solution.py:37
  36.9 2.9 %collective-permute-start.11 = (f32[136,768]{1,0:T(8,128)S(1)}, f32[136,768]{1,0:T(8,128)S(1)}, u32[]{:S(2)}, u32[]{:S(2)}) collective-permute-start(f32[136,768]{1,0:T(8,128)S(1)} %shard_map.51), channel_id=1, source_target_pairs={{0,1},{1,0},{2,3},{3,2},{4,5},{5,4},{6,7},{7,6},{8,9},{9,8},{10,11... | collective-permute-start | bytes 1253384 | tf_op jit(solution)/shard_map/ppermute | solution.py:37

commit v3 on v2

--- a/solution.py
+++ b/solution.py
@@ -16,6 +16,7 @@
 
 WIDE = 8
 LAST = 8
+NEAR = 4
 
 X_FIRST = 1
 
@@ -117,40 +118,41 @@
         doc_start = docs[...]
     first_doc, last_doc = jnp.min(doc_start), jnp.max(doc_start)
 
-    def absorb(tile, starts, masked):
-        keys = len(starts) * chunk
-        key_tile = tile[:, :head_dim]
-        value_t = jnp.concatenate([tile[:, head_dim:].T, jnp.ones((16, keys), tile.dtype)], axis=0)
-        if masked:
-            step = lax.broadcasted_iota(jnp.int32, (chunk, 1), 0)
-            past = jnp.concatenate([step + start for start in starts], axis=0) - doc_start
-            reach = (q_pos - doc_start).astype(jnp.uint32)
-            allowed = past.astype(jnp.uint32) <= reach
-
-        def scores(group, h):
+    def absorb(tiles, masked):
+        keys_of, values_of, allowed = [], [], []
+        for tile, starts in tiles:
+            keys_of.append(tile[:, :head_dim])
+            ones = jnp.ones((16, tile.shape[0]), tile.dtype)
+            values_of.append(jnp.concatenate([tile[:, head_dim:].T, ones], axis=0))
+            if masked:
+                step = lax.broadcasted_iota(jnp.int32, (chunk, 1), 0)
+                past = jnp.concatenate([step + start for start in starts], axis=0) - doc_start
+                allowed.append(past.astype(jnp.uint32) <= (q_pos - doc_start).astype(jnp.uint32))
+
+        def scores(t, group, h):
             return lax.dot_general(
-                key_tile,
+                keys_of[t],
                 q_refs[group][:, h * head_dim : (h + 1) * head_dim],
                 (((1,), (1,)), ((), ())),
                 preferred_element_type=jnp.float32,
             )
 
-        def finish(group, h, p, alpha):
+        def finish(t, group, h, p, alpha):
             ref, cols = state[group], slice(h * rows, (h + 1) * rows)
-            out = jnp.dot(value_t, p, preferred_element_type=jnp.float32)
+            out = jnp.dot(values_of[t], p, preferred_element_type=jnp.float32)
             ref[row_l, cols] = ref[row_l, cols] * alpha + out[head_dim : head_dim + 1]
             ref[:head_dim, cols] = ref[:head_dim, cols] * alpha + out[:head_dim]
 
-        heads = [(group, h) for group in range(groups) for h in range(heads_here)]
-        ahead = [scores(*heads[0]), scores(*heads[1])]
+        units = [(t, group, h) for t in range(len(tiles)) for group in range(groups) for h in range(heads_here)]
+        ahead = [scores(*units[0]), scores(*units[1])]
         waiting = None
-        for j, (group, h) in enumerate(heads):
+        for j, (t, group, h) in enumerate(units):
             ref, cols = state[group], slice(h * rows, (h + 1) * rows)
             s = ahead.pop(0)
-            if j + 2 < len(heads):
-                ahead.append(scores(*heads[j + 2]))
+            if j + 2 < len(units):
+                ahead.append(scores(*units[j + 2]))
             if masked:
-                s = jnp.where(allowed, s, NEG)
+                s = jnp.where(allowed[t], s, NEG)
             m_old = ref[row_m, cols]
             m_new = jnp.maximum(m_old, jnp.max(s, axis=0, keepdims=True))
             alpha = jnp.exp2((m_old - m_new) * scale)
@@ -158,56 +160,47 @@
             ref[row_m, cols] = m_new
             if waiting is not None:
                 finish(*waiting)
-            waiting = (group, h, p, alpha)
+            waiting = (t, group, h, p, alpha)
         finish(*waiting)
 
     def reach_of(starts):
-        needed = full = None
+        needed, full = [], []
         for start in starts:
-            here = (start + (chunk - 1) >= first_doc) & (start <= last_row)
-            whole = (start >= last_doc) & (start + (chunk - 1) <= first_row)
-            needed = here if needed is None else needed | here
-            full = whole if full is None else full & whole
-        return needed, full
-
-    def absorb_if_needed(ref, begin, starts, halves=False):
-        near, far = starts[: len(starts) // 2], starts[len(starts) // 2 :]
-        needed, full = reach_of(starts)
-
-        def part(count):
-            return ref[begin * chunk : (begin + count) * chunk, :]
-
-        @pl.when(full)
+            needed.append((start + (chunk - 1) >= first_doc) & (start <= last_row))
+            full.append((start >= last_doc) & (start + (chunk - 1) <= first_row))
+        return functools.reduce(jnp.logical_or, needed), functools.reduce(jnp.logical_and, full)
+
+    def absorb_needed(parts, may_be_full):
+        needed, full = reach_of([start for _, starts in parts for start in starts])
+        beyond, _ = reach_of([start for _, starts in parts for start in starts[NEAR:]])
+
+        def tiles(count):
+            return [(ref[: len(starts[:count]) * chunk, :], starts[:count]) for ref, starts in parts]
+
+        @pl.when(needed & jnp.logical_not(beyond))
         def _():
-            absorb(part(len(starts)), starts, False)
-
-        if halves:
-            beyond, _ = reach_of(far)
-
-            @pl.when(needed & jnp.logical_not(beyond))
+            near = tiles(NEAR)
+            absorb([(jnp.concatenate([t for t, _ in near], axis=0), [s for _, starts in near for s in starts])], True)
+
+        if may_be_full:
+
+            @pl.when(full)
             def _():
-                absorb(part(len(near)), near, True)
-
-            needed = beyond
-
-        @pl.when(needed & jnp.logical_not(full))
+                absorb(tiles(None), False)
+
+            beyond = beyond & jnp.logical_not(full)
+
+        @pl.when(beyond)
         def _():
-            absorb(part(len(starts)), starts, True)
+            absorb(tiles(None), True)
 
     if "own" in kv:
-        absorb_if_needed(kv["own"], 0, near_starts(core, start_of), True)
-        absorb_if_needed(kv["own"], WIDE, far_starts(core, start_of))
-    half = WIDE // 2
+        absorb_needed([(kv["own"], near_starts(core, start_of) + far_starts(core, start_of))], False)
     if 2 in kv:
-        two = side_starts(core, y, start_of, 2)
-        absorb_if_needed(kv[2], 0, two, True)
-        absorb_if_needed(kv[2], WIDE, [jnp.where(core == X_FIRST, start_of(LAST, 2), FAR)])
-    for by in (1, 3):
-        starts = side_starts(core, y, start_of, by)
-        if (by, 0) in kv:
-            absorb_if_needed(kv[by, 0], 0, starts[:half])
-        if (by, 1) in kv:
-            absorb_if_needed(kv[by, 1], 0, starts[half:])
+        last = jnp.where(core == X_FIRST, start_of(LAST, 2), FAR)
+        absorb_needed([(kv[2], side_starts(core, y, start_of, 2) + [last])], False)
+    if 1 in kv:
+        absorb_needed([(kv[by], side_starts(core, y, start_of, by)) for by in (1, 3)], True)
 
 
 def attend(docs, qs, kv, states, chunk, head_dim, scale):
@@ -292,10 +285,11 @@
     core = lax.axis_index("head") % NC
 
     own = join(key_rows, value_rows)
+    own, late_q = lax.optimization_barrier((own, queries))
     back8 = send(own, later_plane(2))
     back4 = send(own, later_plane(1))
-    back4, back8, late_q = lax.optimization_barrier((back4, back8, queries))
     other_q = send(late_q, other_core)
+    back8, back4, other_q = lax.optimization_barrier((back8, back4, other_q))
 
     def round_x(by):
         return (ctx // 2) % NX + by >= NX
@@ -312,25 +306,16 @@
         held += [plane] + [got[by][i * chunk : (i + 1) * chunk] for by in (1, 2, 3)]
     held = jnp.concatenate(held + [own], axis=0)
 
-    def second(by, first, chunks):
-        begin = jnp.where(core == X_FIRST, ctx % 2 if by != 2 else 0, jnp.where(round_x(by), NY, 0)) + first
+    def second(by, chunks):
+        begin = jnp.where(core == X_FIRST, ctx % 2 if by != 2 else 0, jnp.where(round_x(by), NY, 0))
         return send(lax.dynamic_slice_in_dim(held, begin * chunk, chunks * chunk, 0), second_axis(by))
 
-    half = WIDE // 2
-    sides = {2: second(2, 0, WIDE + 1)}
-    for part in (0, 1):
-        for by in (1, 3):
-            sides[by, part] = second(by, part * half, half)
+    sides = {2: second(2, WIDE + 1), 1: second(1, WIDE), 3: second(3, WIDE)}
+    last = {by: sides[by] for by in (1, 3)}
     call = functools.partial(attend, chunk=chunk, head_dim=head_dim, scale=scale)
     both = [queries, other_q]
     *states, docs = call(doc_lengths, both, {"own": held}, None)
-
-    def some(*keys):
-        return {key: sides[key] for key in keys}
-
-    states = call(docs, both, some(2), states)
-    keep, away = call(docs, both, some((1, 0), (3, 0)), states)
-    last = some((1, 1), (3, 1))
+    keep, away = call(docs, both, {2: sides[2]}, states)
     (away,) = call(docs, [other_q], last, [away])
     came = send(away, other_core)
     (keep,) = call(docs, [queries], last, [keep])

time: 41.1 us -> 40.9 us (level)
  waiting for transfers between devices: 8.49 us -> 13.6 us
  starting transfers between devices: 24.8 us -> 19.7 us
  Pallas kernels: 5.44 us -> 5 us
    ppermute x12 -> x10, waiting for transfers between devices: 8.49 us -> 13.6 us  [send(): return lax.ppermute(array, ('ctx', 'head'), sorted(pairs))]
    ppermute x12 -> x10, starting transfers between devices: 24.8 us -> 19.7 us  [send(): return lax.ppermute(array, ('ctx', 'head'), sorted(pairs))]
    pallas_call x5 -> x4, Pallas kernels: 4.58 us -> 4.12 us  [attend(): pl.pallas_call(functools.partial(attend_kernel, names, len(qs), chunk, sc...]
  transfers between devices with their start and end apart: 12 -> 10, of which waited for: 6 -> 8; matrix products, arithmetic and copies ran while one was open for 0% -> 0% of each run, Pallas kernels for 11% -> 9%
where the time goes in v3:
time: 40.9 us; the launch traced here: 40.3 us
  starting transfers between devices  19.7 us (48%)
  waiting for transfers between devices  13.6 us (33%)
  Pallas kernels  5 us (12%)
  local copies, waits for them, and re-layouts  1.64 us (4%)
    ppermute x10, starting transfers between devices, send(): return lax.ppermute(array, ('ctx', 'head'), sorted(pairs))  19.7 us
    ppermute x10, waiting for transfers between devices, send(): return lax.ppermute(array, ('ctx', 'head'), sorted(pairs))  13.6 us
    pallas_call x4, Pallas kernels, attend(): pl.pallas_call(functools.partial(attend_kernel, names, len(qs), chunk, sc...  4.12 us
    unnamed x19, local copies, waits for them, and re-layouts  1.55 us
    pallas_call x1, Pallas kernels, merge(): pl.pallas_call(functools.partial(merge_kernel, head_dim, scale), out_shap...  0.85 us
  transfers between devices with their start and end apart: 10, of which 8 were waited for; matrix products, arithmetic and copies ran while one was open for 0% of the time, Pallas kernels for 9%

profile of v3, /device:TPU:1, one launch (start us, length us, event | category | flops | bytes accessed | tf_op | source)
XLA Modules:
  0.0 40.3 jit_solution(809199442774274235)
XLA Ops:
  0.0 0.7 %copy-done = bf16[96,128]{1,0:T(8,128)(2,1)S(1)} copy-done((bf16[96,128]{1,0:T(8,128)(2,1)S(1)}, bf16[96,128]{1,0:T(8,128)(2,1)}, u32[]{:S(2)}) %copy-start) | copy-done | bytes 24600
  0.7 0.7 %copy-done.1 = bf16[96,128]{1,0:T(8,128)(2,1)S(1)} copy-done((bf16[96,128]{1,0:T(8,128)(2,1)S(1)}, bf16[96,128]{1,0:T(8,128)(2,1)}, u32[]{:S(2)}) %copy-start.1) | copy-done | bytes 24600
  1.5 3.3 %collective-permute-start.2 = (bf16[384,256]{1,0:T(8,128)(2,1)}, bf16[384,256]{1,0:T(8,128)(2,1)S(1)}, u32[]{:S(2)}, u32[]{:S(2)}) collective-permute-start(bf16[384,256]{1,0:T(8,128)(2,1)} %refs_1_.5), channel_id=1, source_target_pairs={{0,1},{1,0},{2,3},{3,2},{4,5},{5,4},{6,7},{7,6},{8,9},{9,8},{10,11... | collective-permute-start | bytes 589832 | tf_op jit(solution)/shard_map/ppermute | solution.py:38
  4.8 1.3 %collective-permute-start = (bf16[96,256]{1,0:T(8,128)(2,1)S(1)}, bf16[96,256]{1,0:T(8,128)(2,1)S(1)}, u32[]{:S(2)}, u32[]{:S(2)}) collective-permute-start(bf16[96,256]{1,0:T(8,128)(2,1)S(1)} %shard_map.46), channel_id=1, source_target_pairs={{0,64},{1,65},{2,66},{3,67},{4,68},{5,69},{6,70},{7,71},{8,72},{9,... | collective-permute-start | bytes 147464 | tf_op jit(solution)/shard_map/ppermute | solution.py:38
  6.1 1.6 %collective-permute-start.1 = (bf16[96,256]{1,0:T(8,128)(2,1)S(1)}, bf16[96,256]{1,0:T(8,128)(2,1)S(1)}, u32[]{:S(2)}, u32[]{:S(2)}) collective-permute-start(bf16[96,256]{1,0:T(8,128)(2,1)S(1)} %shard_map.46), channel_id=1, source_target_pairs={{0,32},{1,33},{2,34},{3,35},{4,36},{5,37},{6,38},{7,39},{8,40},{9,... | collective-permute-start | bytes 147464 | tf_op jit(solution)/shard_map/ppermute | solution.py:38
  7.8 3.4 %collective-permute-done = bf16[96,256]{1,0:T(8,128)(2,1)S(1)} collective-permute-done((bf16[96,256]{1,0:T(8,128)(2,1)S(1)}, bf16[96,256]{1,0:T(8,128)(2,1)S(1)}, u32[]{:S(2)}, u32[]{:S(2)}) %collective-permute-start) | collective-permute-done | bytes 49184 | tf_op jit(solution)/shard_map/ppermute | solution.py:38
  11.1 1.7 %collective-permute-done.1 = bf16[96,256]{1,0:T(8,128)(2,1)S(1)} collective-permute-done((bf16[96,256]{1,0:T(8,128)(2,1)S(1)}, bf16[96,256]{1,0:T(8,128)(2,1)S(1)}, u32[]{:S(2)}, u32[]{:S(2)}) %collective-permute-start.1) | collective-permute-done | bytes 49184 | tf_op jit(solution)/shard_map/ppermute | solution.py:38
  12.9 1.3 %collective-permute-start.3 = (bf16[288,256]{1,0:T(8,128)(2,1)S(1)}, bf16[288,256]{1,0:T(8,128)(2,1)S(1)}, u32[]{:S(2)}, u32[]{:S(2)}) collective-permute-start(bf16[288,256]{1,0:T(8,128)(2,1)S(1)} %get-tuple-element.35), channel_id=1, source_target_pairs={{0,4},{1,9},{2,6},{3,11},{4,2},{5,13},{6,0},{7,15},{8,12},{9,17},{... | collective-permute-start | bytes 442376 | tf_op jit(solution)/shard_map/ppermute | solution.py:38
  14.2 2.5 %collective-permute-start.4 = (bf16[288,256]{1,0:T(8,128)(2,1)S(1)}, bf16[288,256]{1,0:T(8,128)(2,1)S(1)}, u32[]{:S(2)}, u32[]{:S(2)}) collective-permute-start(bf16[288,256]{1,0:T(8,128)(2,1)S(1)} %get-tuple-element.34), channel_id=1, source_target_pairs={{0,2},{1,17},{2,0},{3,19},{4,6},{5,21},{6,4},{7,23},{8,10},{9,25},... | collective-permute-start | bytes 442376 | tf_op jit(solution)/shard_map/ppermute | solution.py:38
  16.6 1.2 %collective-permute-start.5 = (bf16[288,256]{1,0:T(8,128)(2,1)S(1)}, bf16[288,256]{1,0:T(8,128)(2,1)S(1)}, u32[]{:S(2)}, u32[]{:S(2)}) collective-permute-start(bf16[288,256]{1,0:T(8,128)(2,1)S(1)} %get-tuple-element.33), channel_id=1, source_target_pairs={{0,6},{1,25},{2,4},{3,27},{4,0},{5,29},{6,2},{7,31},{8,14},{9,1},{... | collective-permute-start | bytes 442376 | tf_op jit(solution)/shard_map/ppermute | solution.py:38
  17.8 0.7 %collective-permute-done.3 = bf16[288,256]{1,0:T(8,128)(2,1)S(1)} collective-permute-done((bf16[288,256]{1,0:T(8,128)(2,1)S(1)}, bf16[288,256]{1,0:T(8,128)(2,1)S(1)}, u32[]{:S(2)}, u32[]{:S(2)}) %collective-permute-start.3) | collective-permute-done | bytes 147488 | tf_op jit(solution)/shard_map/ppermute | solution.py:38
  18.5 2.6 %collective-permute-done.4 = bf16[288,256]{1,0:T(8,128)(2,1)S(1)} collective-permute-done((bf16[288,256]{1,0:T(8,128)(2,1)S(1)}, bf16[288,256]{1,0:T(8,128)(2,1)S(1)}, u32[]{:S(2)}, u32[]{:S(2)}) %collective-permute-start.4) | collective-permute-done | bytes 147488 | tf_op jit(solution)/shard_map/ppermute | solution.py:38
  21.3 2.9 %collective-permute-start.8 = (bf16[864,256]{1,0:T(8,128)(2,1)S(1)}, bf16[864,256]{1,0:T(8,128)(2,1)S(1)}, u32[]{:S(2)}, u32[]{:S(2)}) collective-permute-start(bf16[864,256]{1,0:T(8,128)(2,1)S(1)} %constant_dynamic-slice_fusion), channel_id=1, source_target_pairs={{0,16},{1,3},{2,18},{3,1},{4,20},{5,7},{6,22},{7,5},{8,24},{9,11},... | collective-permute-start | bytes 1327112 | tf_op jit(solution)/shard_map/ppermute | solution.py:38
  24.2 0.5 %collective-permute-start.6 = (bf16[768,256]{1,0:T(8,128)(2,1)S(1)}, bf16[768,256]{1,0:T(8,128)(2,1)S(1)}, u32[]{:S(2)}, u32[]{:S(2)}) collective-permute-start(bf16[768,256]{1,0:T(8,128)(2,1)S(1)} %get-tuple-element.26), channel_id=1, source_target_pairs={{0,8},{1,5},{2,10},{3,7},{4,12},{5,3},{6,14},{7,1},{8,16},{9,13},{... | collective-permute-start | bytes 1179656 | tf_op jit(solution)/shard_map/ppermute | solution.py:38
  24.7 2.3 %collective-permute-start.7 = (bf16[768,256]{1,0:T(8,128)(2,1)S(1)}, bf16[768,256]{1,0:T(8,128)(2,1)S(1)}, u32[]{:S(2)}, u32[]{:S(2)}) collective-permute-start(bf16[768,256]{1,0:T(8,128)(2,1)S(1)} %get-tuple-element.25), channel_id=1, source_target_pairs={{0,24},{1,7},{2,26},{3,5},{4,28},{5,1},{6,30},{7,3},{8,0},{9,15},{... | collective-permute-start | bytes 1179656 | tf_op jit(solution)/shard_map/ppermute | solution.py:38
  26.9 2.0 %shard_map.47 = (f32[136,768]{1,0:T(8,128)S(1)}, f32[136,768]{1,0:T(8,128)S(1)}, s32[1,384]{1,0:T(1,128)S(1)}) custom-call(s32[64]{0:T(128)S(1)} %copy-done.3, bf16[384,256]{1,0:T(8,128)(2,1)S(1)} %copy-done.2, bf16[384,256]{1,0:T(8,128)(2,1)S(1)} %collective-permute-done.2.refs_2_.refs_1_, bf16[1248,256]{1,0:T(8,128)(2,1)S(1)} %constant_dynamic-update-slice_fusion.refs_3_), custom_call_target="tpu_custom_call" | custom-call | flops 981467136 | bytes 393216 | tf_op jit(solution)/shard_map/pallas_call | solution.py:216
  28.9 1.4 %collective-permute-done.8.refs_3_ = bf16[864,256]{1,0:T(8,128)(2,1)S(1)} collective-permute-done((bf16[864,256]{1,0:T(8,128)(2,1)S(1)}, bf16[864,256]{1,0:T(8,128)(2,1)S(1)}, u32[]{:S(2)}, u32[]{:S(2)}) %collective-permute-start.8) | collective-permute-done | bytes 442400 | tf_op jit(solution)/shard_map/ppermute | solution.py:38
  30.3 1.6 %shard_map.48 = (f32[136,768]{1,0:T(8,128)S(1)}, f32[136,768]{1,0:T(8,128)S(1)}) custom-call(s32[1,384]{1,0:T(1,128)S(1)} %get-tuple-element.20.refs_0_, bf16[384,256]{1,0:T(8,128)(2,1)S(1)} %copy-done.2, bf16[384,256]{1,0:T(8,128)(2,1)S(1)} %collective-permute-done.2.refs_2_.refs_1_, bf16[864,256]{1,0:T(8,128)(2,1)S(1)} %collective-permute-done.8.refs_3_, ...), custom_call_target="tpu_custom_call" | custom-call | flops 679477248 | bytes 393216 | tf_op jit(solution)/shard_map/pallas_call | solution.py:216
  31.9 2.6 %collective-permute-done.6.refs_2_ = bf16[768,256]{1,0:T(8,128)(2,1)S(1)} collective-permute-done((bf16[768,256]{1,0:T(8,128)(2,1)S(1)}, bf16[768,256]{1,0:T(8,128)(2,1)S(1)}, u32[]{:S(2)}, u32[]{:S(2)}) %collective-permute-start.6) | collective-permute-done | bytes 393248 | tf_op jit(solution)/shard_map/ppermute | solution.py:38
  34.8 0.3 shard_map.50
  35.1 3.0 %collective-permute-start.9 = (f32[136,768]{1,0:T(8,128)S(1)}, f32[136,768]{1,0:T(8,128)S(1)}, u32[]{:S(2)}, u32[]{:S(2)}) collective-permute-start(f32[136,768]{1,0:T(8,128)S(1)} %shard_map.50), channel_id=1, source_target_pairs={{0,1},{1,0},{2,3},{3,2},{4,5},{5,4},{6,7},{7,6},{8,9},{9,8},{10,11... | collective-permute-start | bytes 1253384 | tf_op jit(solution)/shard_map/ppermute | solution.py:38
  38.0 0.3 shard_map.49.keep_ref
  38.3 1.1 %collective-permute-done.9.came_ref = f32[136,768]{1,0:T(8,128)S(1)} collective-permute-done((f32[136,768]{1,0:T(8,128)S(1)}, f32[136,768]{1,0:T(8,128)S(1)}, u32[]{:S(2)}, u32[]{:S(2)}) %collective-permute-start.9) | collective-permute-done | bytes 417824 | tf_op jit(solution)/shard_map/ppermute | solution.py:38
  39.4 0.8 %shard_map.51 = bf16[384,256]{1,0:T(8,128)(2,1)} custom-call(f32[136,768]{1,0:T(8,128)S(1)} %shard_map.49.keep_ref, f32[136,768]{1,0:T(8,128)S(1)} %collective-permute-done.9.came_ref), custom_call_target="tpu_custom_call" | custom-call | tf_op jit(solution)/shard_map/pallas_call | solution.py:271
  (26 shorter events, 0.5 us)
Async XLA Ops:
  0.0 0.7 %copy-start = (bf16[96,128]{1,0:T(8,128)(2,1)S(1)}, bf16[96,128]{1,0:T(8,128)(2,1)}, u32[]{:S(2)}) copy-start(bf16[96,128]{1,0:T(8,128)(2,1)} %k_ref.1) | copy-start | bytes 73732
  0.7 0.7 %copy-start.1 = (bf16[96,128]{1,0:T(8,128)(2,1)S(1)}, bf16[96,128]{1,0:T(8,128)(2,1)}, u32[]{:S(2)}) copy-start(bf16[96,128]{1,0:T(8,128)(2,1)} %v_ref.1) | copy-start | bytes 73732
  1.5 11.3 %collective-permute-start.2 = (bf16[384,256]{1,0:T(8,128)(2,1)}, bf16[384,256]{1,0:T(8,128)(2,1)S(1)}, u32[]{:S(2)}, u32[]{:S(2)}) collective-permute-start(bf16[384,256]{1,0:T(8,128)(2,1)} %refs_1_.5), channel_id=1, source_target_pairs={{0,1},{1,0},{2,3},{3,2},{4,5},{5,4},{6,7},{7,6},{8,9},{9,8},{10,11... | collective-permute-start | bytes 589832 | tf_op jit(solution)/shard_map/ppermute | solution.py:38
  4.8 6.3 %collective-permute-start = (bf16[96,256]{1,0:T(8,128)(2,1)S(1)}, bf16[96,256]{1,0:T(8,128)(2,1)S(1)}, u32[]{:S(2)}, u32[]{:S(2)}) collective-permute-start(bf16[96,256]{1,0:T(8,128)(2,1)S(1)} %shard_map.46), channel_id=1, source_target_pairs={{0,64},{1,65},{2,66},{3,67},{4,68},{5,69},{6,70},{7,71},{8,72},{9,... | collective-permute-start | bytes 147464 | tf_op jit(solution)/shard_map/ppermute | solution.py:38
  6.1 6.7 %collective-permute-start.1 = (bf16[96,256]{1,0:T(8,128)(2,1)S(1)}, bf16[96,256]{1,0:T(8,128)(2,1)S(1)}, u32[]{:S(2)}, u32[]{:S(2)}) collective-permute-start(bf16[96,256]{1,0:T(8,128)(2,1)S(1)} %shard_map.46), channel_id=1, source_target_pairs={{0,32},{1,33},{2,34},{3,35},{4,36},{5,37},{6,38},{7,39},{8,40},{9,... | collective-permute-start | bytes 147464 | tf_op jit(solution)/shard_map/ppermute | solution.py:38
  12.9 5.6 %collective-permute-start.3 = (bf16[288,256]{1,0:T(8,128)(2,1)S(1)}, bf16[288,256]{1,0:T(8,128)(2,1)S(1)}, u32[]{:S(2)}, u32[]{:S(2)}) collective-permute-start(bf16[288,256]{1,0:T(8,128)(2,1)S(1)} %get-tuple-element.35), channel_id=1, source_target_pairs={{0,4},{1,9},{2,6},{3,11},{4,2},{5,13},{6,0},{7,15},{8,12},{9,17},{... | collective-permute-start | bytes 442376 | tf_op jit(solution)/shard_map/ppermute | solution.py:38
  14.2 6.9 %collective-permute-start.4 = (bf16[288,256]{1,0:T(8,128)(2,1)S(1)}, bf16[288,256]{1,0:T(8,128)(2,1)S(1)}, u32[]{:S(2)}, u32[]{:S(2)}) collective-permute-start(bf16[288,256]{1,0:T(8,128)(2,1)S(1)} %get-tuple-element.34), channel_id=1, source_target_pairs={{0,2},{1,17},{2,0},{3,19},{4,6},{5,21},{6,4},{7,23},{8,10},{9,25},... | collective-permute-start | bytes 442376 | tf_op jit(solution)/shard_map/ppermute | solution.py:38
  16.6 4.4 %collective-permute-start.5 = (bf16[288,256]{1,0:T(8,128)(2,1)S(1)}, bf16[288,256]{1,0:T(8,128)(2,1)S(1)}, u32[]{:S(2)}, u32[]{:S(2)}) collective-permute-start(bf16[288,256]{1,0:T(8,128)(2,1)S(1)} %get-tuple-element.33), channel_id=1, source_target_pairs={{0,6},{1,25},{2,4},{3,27},{4,0},{5,29},{6,2},{7,31},{8,14},{9,1},{... | collective-permute-start | bytes 442376 | tf_op jit(solution)/shard_map/ppermute | solution.py:38
  21.2 5.7 %copy-start.2 = (bf16[384,256]{1,0:T(8,128)(2,1)S(1)}, bf16[384,256]{1,0:T(8,128)(2,1)}, u32[]{:S(2)}) copy-start(bf16[384,256]{1,0:T(8,128)(2,1)} %refs_1_.5) | copy-start | bytes 589828
  21.3 9.1 %collective-permute-start.8 = (bf16[864,256]{1,0:T(8,128)(2,1)S(1)}, bf16[864,256]{1,0:T(8,128)(2,1)S(1)}, u32[]{:S(2)}, u32[]{:S(2)}) collective-permute-start(bf16[864,256]{1,0:T(8,128)(2,1)S(1)} %constant_dynamic-slice_fusion), channel_id=1, source_target_pairs={{0,16},{1,3},{2,18},{3,1},{4,20},{5,7},{6,22},{7,5},{8,24},{9,11},... | collective-permute-start | bytes 1327112 | tf_op jit(solution)/shard_map/ppermute | solution.py:38
  24.2 2.8 %copy-start.3 = (s32[64]{0:T(128)S(1)}, s32[64]{0:T(128)}, u32[]{:S(2)}) copy-start(s32[64]{0:T(128)} %refs_0_.1) | copy-start | bytes 772
  24.2 10.3 %collective-permute-start.6 = (bf16[768,256]{1,0:T(8,128)(2,1)S(1)}, bf16[768,256]{1,0:T(8,128)(2,1)S(1)}, u32[]{:S(2)}, u32[]{:S(2)}) collective-permute-start(bf16[768,256]{1,0:T(8,128)(2,1)S(1)} %get-tuple-element.26), channel_id=1, source_target_pairs={{0,8},{1,5},{2,10},{3,7},{4,12},{5,3},{6,14},{7,1},{8,16},{9,13},{... | collective-permute-start | bytes 1179656 | tf_op jit(solution)/shard_map/ppermute | solution.py:38
  24.7 10.1 %collective-permute-start.7 = (bf16[768,256]{1,0:T(8,128)(2,1)S(1)}, bf16[768,256]{1,0:T(8,128)(2,1)S(1)}, u32[]{:S(2)}, u32[]{:S(2)}) collective-permute-start(bf16[768,256]{1,0:T(8,128)(2,1)S(1)} %get-tuple-element.25), channel_id=1, source_target_pairs={{0,24},{1,7},{2,26},{3,5},{4,28},{5,1},{6,30},{7,3},{8,0},{9,15},{... | collective-permute-start | bytes 1179656 | tf_op jit(solution)/shard_map/ppermute | solution.py:38
  35.1 4.4 %collective-permute-start.9 = (f32[136,768]{1,0:T(8,128)S(1)}, f32[136,768]{1,0:T(8,128)S(1)}, u32[]{:S(2)}, u32[]{:S(2)}) collective-permute-start(f32[136,768]{1,0:T(8,128)S(1)} %shard_map.50), channel_id=1, source_target_pairs={{0,1},{1,0},{2,3},{3,2},{4,5},{5,4},{6,7},{7,6},{8,9},{9,8},{10,11... | collective-permute-start | bytes 1253384 | tf_op jit(solution)/shard_map/ppermute | solution.py:38

commit v4 on v3

--- a/solution.py
+++ b/solution.py
@@ -170,12 +170,22 @@
             full.append((start >= last_doc) & (start + (chunk - 1) <= first_row))
         return functools.reduce(jnp.logical_or, needed), functools.reduce(jnp.logical_and, full)
 
-    def absorb_needed(parts, may_be_full):
+    def absorb_needed(parts, may_be_full, choose=None):
         needed, full = reach_of([start for _, starts in parts for start in starts])
         beyond, _ = reach_of([start for _, starts in parts for start in starts[NEAR:]])
 
         def tiles(count):
             return [(ref[: len(starts[:count]) * chunk, :], starts[:count]) for ref, starts in parts]
+
+        if choose is not None:
+            picked, places, rest = choose(parts)
+            more, _ = reach_of(rest)
+
+            @pl.when(needed & jnp.logical_not(more))
+            def _():
+                absorb([(picked(), places)], True)
+
+            needed = more
 
         @pl.when(needed & jnp.logical_not(beyond))
         def _():
@@ -193,6 +203,17 @@
         @pl.when(beyond)
         def _():
             absorb(tiles(None), True)
+
+    def nearest(parts):
+        (ref, starts), (back_ref, back_starts) = parts
+        pick = [jnp.where(core == X_FIRST, a, b) for a, b in zip(back_starts[:2], starts[2:4])]
+        left = [jnp.where(core == X_FIRST, b, a) for a, b in zip(back_starts[:2], starts[2:4])]
+
+        def tile():
+            other = jnp.where(core == X_FIRST, back_ref[: 2 * chunk, :], ref[2 * chunk : 4 * chunk, :])
+            return jnp.concatenate([ref[: 2 * chunk, :], other], axis=0)
+
+        return tile, starts[:2] + pick, starts[4:] + back_starts[2:] + left
 
     if "own" in kv:
         absorb_needed([(kv["own"], near_starts(core, start_of) + far_starts(core, start_of))], False)
@@ -200,7 +221,7 @@
         last = jnp.where(core == X_FIRST, start_of(LAST, 2), FAR)
         absorb_needed([(kv[2], side_starts(core, y, start_of, 2) + [last])], False)
     if 1 in kv:
-        absorb_needed([(kv[by], side_starts(core, y, start_of, by)) for by in (1, 3)], True)
+        absorb_needed([(kv[by], side_starts(core, y, start_of, by)) for by in (1, 3)], True, nearest)
 
 
 def attend(docs, qs, kv, states, chunk, head_dim, scale):
@@ -227,30 +248,6 @@
     )(docs, *qs, *arrays, *given)
 
 
-def join_kernel(k_ref, v_ref, out_ref, sems):
-    head_dim = k_ref.shape[1]
-    copies = [
-        pltpu.make_async_copy(k_ref, out_ref.at[:, :head_dim], sems.at[0]),
-        pltpu.make_async_copy(v_ref, out_ref.at[:, head_dim:], sems.at[1]),
-    ]
-    for copy in copies:
-        copy.start()
-    for copy in copies:
-        copy.wait()
-
-
-def join(key_rows, value_rows):
-    chunk, head_dim = key_rows.shape
-    return pl.pallas_call(
-        join_kernel,
-        out_shape=jax.ShapeDtypeStruct((chunk, 2 * head_dim), key_rows.dtype),
-        in_specs=[pl.BlockSpec(memory_space=pltpu.HBM)] * 2,
-        out_specs=pl.BlockSpec(memory_space=pltpu.VMEM),
-        scratch_shapes=[pltpu.SemaphoreType.DMA((2,))],
-        compiler_params=pltpu.CompilerParams(vmem_limit_bytes=4 * 1024 * 1024),
-    )(key_rows, value_rows)
-
-
 def merge_kernel(head_dim, scale, keep_ref, came_ref, out_ref):
     rows = out_ref.shape[0]
     for h in range(out_ref.shape[1] // head_dim):
@@ -284,7 +281,7 @@
     ctx = lax.axis_index("ctx")
     core = lax.axis_index("head") % NC
 
-    own = join(key_rows, value_rows)
+    own = jnp.concatenate([key_rows, value_rows], axis=1)
     own, late_q = lax.optimization_barrier((own, queries))
     back8 = send(own, later_plane(2))
     back4 = send(own, later_plane(1))

time: 40.9 us -> 39.7 us (0.971); the launches traced: 40.3 us -> 39.5 us
  local copies, waits for them, and re-layouts: 1.64 us -> 0.17 us
  other arithmetic: 0.08 us -> 0.84 us
    unnamed x19 -> x15, local copies, waits for them, and re-layouts: 1.55 us -> 0.07 us
    concatenate x0 -> x1, other arithmetic: none -> 0.76 us  [on_device(): own = jnp.concatenate([key_rows, value_rows], axis=1)]
  transfers between devices with their start and end apart: 10 -> 10, of which waited for: 8 -> 8; matrix products, arithmetic and copies ran while one was open for 0% -> 0% of each run, Pallas kernels for 9% -> 10%
where the time goes in v4:
time: 39.7 us; the launch traced here: 39.5 us
  starting transfers between devices  19.7 us (50%)
  waiting for transfers between devices  13.6 us (34%)
  Pallas kernels  5.01 us (13%)
  other arithmetic  0.84 us (2%)
    ppermute x10, starting transfers between devices, send(): return lax.ppermute(array, ('ctx', 'head'), sorted(pairs))  19.7 us
    ppermute x10, waiting for transfers between devices, send(): return lax.ppermute(array, ('ctx', 'head'), sorted(pairs))  13.6 us
    pallas_call x4, Pallas kernels, attend(): pl.pallas_call(functools.partial(attend_kernel, names, len(qs), chunk, sc...  4.16 us
    pallas_call x1, Pallas kernels, merge(): pl.pallas_call(functools.partial(merge_kernel, head_dim, scale), out_shap...  0.85 us
  transfers between devices with their start and end apart: 10, of which 8 were waited for; matrix products, arithmetic and copies ran while one was open for 0% of the time, Pallas kernels for 10%

profile of v4, /device:TPU:1, one launch (start us, length us, event | category | flops | bytes accessed | tf_op | source)
XLA Modules:
  0.0 39.5 jit_solution(10831478715918932370)
XLA Ops:
  0.0 0.8 %pad_maximum_fusion.3 = bf16[96,256]{1,0:T(8,128)(2,1)S(1)} fusion(bf16[96,128]{1,0:T(8,128)(2,1)} %param.6, bf16[96,128]{1,0:T(8,128)(2,1)} %param.5), kind=kLoop, calls=%fused_computation.12 | loop fusion | flops 98304 | bytes 98304 | tf_op jit(solution)/shard_map/concatenate | solution.py:284
  0.8 3.3 %collective-permute-start.2 = (bf16[384,256]{1,0:T(8,128)(2,1)}, bf16[384,256]{1,0:T(8,128)(2,1)S(1)}, u32[]{:S(2)}, u32[]{:S(2)}) collective-permute-start(bf16[384,256]{1,0:T(8,128)(2,1)} %refs_1_.5), channel_id=1, source_target_pairs={{0,1},{1,0},{2,3},{3,2},{4,5},{5,4},{6,7},{7,6},{8,9},{9,8},{10,11... | collective-permute-start | bytes 589832 | tf_op jit(solution)/shard_map/ppermute | solution.py:38
  4.1 1.3 %collective-permute-start = (bf16[96,256]{1,0:T(8,128)(2,1)S(1)}, bf16[96,256]{1,0:T(8,128)(2,1)S(1)}, u32[]{:S(2)}, u32[]{:S(2)}) collective-permute-start(bf16[96,256]{1,0:T(8,128)(2,1)S(1)} %pad_maximum_fusion.3), channel_id=1, source_target_pairs={{0,64},{1,65},{2,66},{3,67},{4,68},{5,69},{6,70},{7,71},{8,72},{9,... | collective-permute-start | bytes 147464 | tf_op jit(solution)/shard_map/ppermute | solution.py:38
  5.3 1.6 %collective-permute-start.1 = (bf16[96,256]{1,0:T(8,128)(2,1)S(1)}, bf16[96,256]{1,0:T(8,128)(2,1)S(1)}, u32[]{:S(2)}, u32[]{:S(2)}) collective-permute-start(bf16[96,256]{1,0:T(8,128)(2,1)S(1)} %pad_maximum_fusion.3), channel_id=1, source_target_pairs={{0,32},{1,33},{2,34},{3,35},{4,36},{5,37},{6,38},{7,39},{8,40},{9,... | collective-permute-start | bytes 147464 | tf_op jit(solution)/shard_map/ppermute | solution.py:38
  7.0 3.4 %collective-permute-done = bf16[96,256]{1,0:T(8,128)(2,1)S(1)} collective-permute-done((bf16[96,256]{1,0:T(8,128)(2,1)S(1)}, bf16[96,256]{1,0:T(8,128)(2,1)S(1)}, u32[]{:S(2)}, u32[]{:S(2)}) %collective-permute-start) | collective-permute-done | bytes 49184 | tf_op jit(solution)/shard_map/ppermute | solution.py:38
  10.4 1.7 %collective-permute-done.1 = bf16[96,256]{1,0:T(8,128)(2,1)S(1)} collective-permute-done((bf16[96,256]{1,0:T(8,128)(2,1)S(1)}, bf16[96,256]{1,0:T(8,128)(2,1)S(1)}, u32[]{:S(2)}, u32[]{:S(2)}) %collective-permute-start.1) | collective-permute-done | bytes 49184 | tf_op jit(solution)/shard_map/ppermute | solution.py:38
  12.1 1.3 %collective-permute-start.3 = (bf16[288,256]{1,0:T(8,128)(2,1)S(1)}, bf16[288,256]{1,0:T(8,128)(2,1)S(1)}, u32[]{:S(2)}, u32[]{:S(2)}) collective-permute-start(bf16[288,256]{1,0:T(8,128)(2,1)S(1)} %get-tuple-element.35), channel_id=1, source_target_pairs={{0,4},{1,9},{2,6},{3,11},{4,2},{5,13},{6,0},{7,15},{8,12},{9,17},{... | collective-permute-start | bytes 442376 | tf_op jit(solution)/shard_map/ppermute | solution.py:38
  13.4 2.5 %collective-permute-start.4 = (bf16[288,256]{1,0:T(8,128)(2,1)S(1)}, bf16[288,256]{1,0:T(8,128)(2,1)S(1)}, u32[]{:S(2)}, u32[]{:S(2)}) collective-permute-start(bf16[288,256]{1,0:T(8,128)(2,1)S(1)} %get-tuple-element.34), channel_id=1, source_target_pairs={{0,2},{1,17},{2,0},{3,19},{4,6},{5,21},{6,4},{7,23},{8,10},{9,25},... | collective-permute-start | bytes 442376 | tf_op jit(solution)/shard_map/ppermute | solution.py:38
  15.9 1.2 %collective-permute-start.5 = (bf16[288,256]{1,0:T(8,128)(2,1)S(1)}, bf16[288,256]{1,0:T(8,128)(2,1)S(1)}, u32[]{:S(2)}, u32[]{:S(2)}) collective-permute-start(bf16[288,256]{1,0:T(8,128)(2,1)S(1)} %get-tuple-element.33), channel_id=1, source_target_pairs={{0,6},{1,25},{2,4},{3,27},{4,0},{5,29},{6,2},{7,31},{8,14},{9,1},{... | collective-permute-start | bytes 442376 | tf_op jit(solution)/shard_map/ppermute | solution.py:38
  17.0 0.7 %collective-permute-done.3 = bf16[288,256]{1,0:T(8,128)(2,1)S(1)} collective-permute-done((bf16[288,256]{1,0:T(8,128)(2,1)S(1)}, bf16[288,256]{1,0:T(8,128)(2,1)S(1)}, u32[]{:S(2)}, u32[]{:S(2)}) %collective-permute-start.3) | collective-permute-done | bytes 147488 | tf_op jit(solution)/shard_map/ppermute | solution.py:38
  17.7 2.6 %collective-permute-done.4 = bf16[288,256]{1,0:T(8,128)(2,1)S(1)} collective-permute-done((bf16[288,256]{1,0:T(8,128)(2,1)S(1)}, bf16[288,256]{1,0:T(8,128)(2,1)S(1)}, u32[]{:S(2)}, u32[]{:S(2)}) %collective-permute-start.4) | collective-permute-done | bytes 147488 | tf_op jit(solution)/shard_map/ppermute | solution.py:38
  20.5 2.9 %collective-permute-start.8 = (bf16[864,256]{1,0:T(8,128)(2,1)S(1)}, bf16[864,256]{1,0:T(8,128)(2,1)S(1)}, u32[]{:S(2)}, u32[]{:S(2)}) collective-permute-start(bf16[864,256]{1,0:T(8,128)(2,1)S(1)} %constant_dynamic-slice_fusion), channel_id=1, source_target_pairs={{0,16},{1,3},{2,18},{3,1},{4,20},{5,7},{6,22},{7,5},{8,24},{9,11},... | collective-permute-start | bytes 1327112 | tf_op jit(solution)/shard_map/ppermute | solution.py:38
  23.4 0.5 %collective-permute-start.6 = (bf16[768,256]{1,0:T(8,128)(2,1)S(1)}, bf16[768,256]{1,0:T(8,128)(2,1)S(1)}, u32[]{:S(2)}, u32[]{:S(2)}) collective-permute-start(bf16[768,256]{1,0:T(8,128)(2,1)S(1)} %get-tuple-element.26), channel_id=1, source_target_pairs={{0,8},{1,5},{2,10},{3,7},{4,12},{5,3},{6,14},{7,1},{8,16},{9,13},{... | collective-permute-start | bytes 1179656 | tf_op jit(solution)/shard_map/ppermute | solution.py:38
  23.9 2.3 %collective-permute-start.7 = (bf16[768,256]{1,0:T(8,128)(2,1)S(1)}, bf16[768,256]{1,0:T(8,128)(2,1)S(1)}, u32[]{:S(2)}, u32[]{:S(2)}) collective-permute-start(bf16[768,256]{1,0:T(8,128)(2,1)S(1)} %get-tuple-element.25), channel_id=1, source_target_pairs={{0,24},{1,7},{2,26},{3,5},{4,28},{5,1},{6,30},{7,3},{8,0},{9,15},{... | collective-permute-start | bytes 1179656 | tf_op jit(solution)/shard_map/ppermute | solution.py:38
  26.2 2.0 %shard_map.46 = (f32[136,768]{1,0:T(8,128)S(1)}, f32[136,768]{1,0:T(8,128)S(1)}, s32[1,384]{1,0:T(1,128)S(1)}) custom-call(s32[64]{0:T(128)S(1)} %copy-done.1, bf16[384,256]{1,0:T(8,128)(2,1)S(1)} %copy-done, bf16[384,256]{1,0:T(8,128)(2,1)S(1)} %collective-permute-done.2.refs_2_.refs_1_, bf16[1248,256]{1,0:T(8,128)(2,1)S(1)} %constant_dynamic-update-slice_fusion.refs_3_), custom_call_target="tpu_custom_call" | custom-call | flops 981467136 | bytes 393216 | tf_op jit(solution)/shard_map/pallas_call | solution.py:237
  28.2 1.4 %collective-permute-done.8.refs_3_ = bf16[864,256]{1,0:T(8,128)(2,1)S(1)} collective-permute-done((bf16[864,256]{1,0:T(8,128)(2,1)S(1)}, bf16[864,256]{1,0:T(8,128)(2,1)S(1)}, u32[]{:S(2)}, u32[]{:S(2)}) %collective-permute-start.8) | collective-permute-done | bytes 442400 | tf_op jit(solution)/shard_map/ppermute | solution.py:38
  29.6 1.5 %shard_map.47 = (f32[136,768]{1,0:T(8,128)S(1)}, f32[136,768]{1,0:T(8,128)S(1)}) custom-call(s32[1,384]{1,0:T(1,128)S(1)} %get-tuple-element.20.refs_0_, bf16[384,256]{1,0:T(8,128)(2,1)S(1)} %copy-done, bf16[384,256]{1,0:T(8,128)(2,1)S(1)} %collective-permute-done.2.refs_2_.refs_1_, bf16[864,256]{1,0:T(8,128)(2,1)S(1)} %collective-permute-done.8.refs_3_, ...), custom_call_target="tpu_custom_call" | custom-call | flops 679477248 | bytes 393216 | tf_op jit(solution)/shard_map/pallas_call | solution.py:237
  31.1 2.6 %collective-permute-done.6.refs_2_ = bf16[768,256]{1,0:T(8,128)(2,1)S(1)} collective-permute-done((bf16[768,256]{1,0:T(8,128)(2,1)S(1)}, bf16[768,256]{1,0:T(8,128)(2,1)S(1)}, u32[]{:S(2)}, u32[]{:S(2)}) %collective-permute-start.6) | collective-permute-done | bytes 393248 | tf_op jit(solution)/shard_map/ppermute | solution.py:38
  33.7 0.2 collective-permute-done.7.refs_3_
  34.0 0.3 shard_map.49
  34.3 3.0 %collective-permute-start.9 = (f32[136,768]{1,0:T(8,128)S(1)}, f32[136,768]{1,0:T(8,128)S(1)}, u32[]{:S(2)}, u32[]{:S(2)}) collective-permute-start(f32[136,768]{1,0:T(8,128)S(1)} %shard_map.49), channel_id=1, source_target_pairs={{0,1},{1,0},{2,3},{3,2},{4,5},{5,4},{6,7},{7,6},{8,9},{9,8},{10,11... | collective-permute-start | bytes 1253384 | tf_op jit(solution)/shard_map/ppermute | solution.py:38
  37.3 0.3 shard_map.48.keep_ref
  37.6 1.1 %collective-permute-done.9.came_ref = f32[136,768]{1,0:T(8,128)S(1)} collective-permute-done((f32[136,768]{1,0:T(8,128)S(1)}, f32[136,768]{1,0:T(8,128)S(1)}, u32[]{:S(2)}, u32[]{:S(2)}) %collective-permute-start.9) | collective-permute-done | bytes 417824 | tf_op jit(solution)/shard_map/ppermute | solution.py:38
  38.7 0.8 %shard_map.50 = bf16[384,256]{1,0:T(8,128)(2,1)} custom-call(f32[136,768]{1,0:T(8,128)S(1)} %shard_map.48.keep_ref, f32[136,768]{1,0:T(8,128)S(1)} %collective-permute-done.9.came_ref), custom_call_target="tpu_custom_call" | custom-call | tf_op jit(solution)/shard_map/pallas_call | solution.py:268
  (22 shorter events, 0.3 us)
Async XLA Ops:
  0.8 11.3 %collective-permute-start.2 = (bf16[384,256]{1,0:T(8,128)(2,1)}, bf16[384,256]{1,0:T(8,128)(2,1)S(1)}, u32[]{:S(2)}, u32[]{:S(2)}) collective-permute-start(bf16[384,256]{1,0:T(8,128)(2,1)} %refs_1_.5), channel_id=1, source_target_pairs={{0,1},{1,0},{2,3},{3,2},{4,5},{5,4},{6,7},{7,6},{8,9},{9,8},{10,11... | collective-permute-start | bytes 589832 | tf_op jit(solution)/shard_map/ppermute | solution.py:38
  4.1 6.3 %collective-permute-start = (bf16[96,256]{1,0:T(8,128)(2,1)S(1)}, bf16[96,256]{1,0:T(8,128)(2,1)S(1)}, u32[]{:S(2)}, u32[]{:S(2)}) collective-permute-start(bf16[96,256]{1,0:T(8,128)(2,1)S(1)} %pad_maximum_fusion.3), channel_id=1, source_target_pairs={{0,64},{1,65},{2,66},{3,67},{4,68},{5,69},{6,70},{7,71},{8,72},{9,... | collective-permute-start | bytes 147464 | tf_op jit(solution)/shard_map/ppermute | solution.py:38
  5.3 6.7 %collective-permute-start.1 = (bf16[96,256]{1,0:T(8,128)(2,1)S(1)}, bf16[96,256]{1,0:T(8,128)(2,1)S(1)}, u32[]{:S(2)}, u32[]{:S(2)}) collective-permute-start(bf16[96,256]{1,0:T(8,128)(2,1)S(1)} %pad_maximum_fusion.3), channel_id=1, source_target_pairs={{0,32},{1,33},{2,34},{3,35},{4,36},{5,37},{6,38},{7,39},{8,40},{9,... | collective-permute-start | bytes 147464 | tf_op jit(solution)/shard_map/ppermute | solution.py:38
  12.1 5.6 %collective-permute-start.3 = (bf16[288,256]{1,0:T(8,128)(2,1)S(1)}, bf16[288,256]{1,0:T(8,128)(2,1)S(1)}, u32[]{:S(2)}, u32[]{:S(2)}) collective-permute-start(bf16[288,256]{1,0:T(8,128)(2,1)S(1)} %get-tuple-element.35), channel_id=1, source_target_pairs={{0,4},{1,9},{2,6},{3,11},{4,2},{5,13},{6,0},{7,15},{8,12},{9,17},{... | collective-permute-start | bytes 442376 | tf_op jit(solution)/shard_map/ppermute | solution.py:38
  13.4 6.9 %collective-permute-start.4 = (bf16[288,256]{1,0:T(8,128)(2,1)S(1)}, bf16[288,256]{1,0:T(8,128)(2,1)S(1)}, u32[]{:S(2)}, u32[]{:S(2)}) collective-permute-start(bf16[288,256]{1,0:T(8,128)(2,1)S(1)} %get-tuple-element.34), channel_id=1, source_target_pairs={{0,2},{1,17},{2,0},{3,19},{4,6},{5,21},{6,4},{7,23},{8,10},{9,25},... | collective-permute-start | bytes 442376 | tf_op jit(solution)/shard_map/ppermute | solution.py:38
  15.9 4.4 %collective-permute-start.5 = (bf16[288,256]{1,0:T(8,128)(2,1)S(1)}, bf16[288,256]{1,0:T(8,128)(2,1)S(1)}, u32[]{:S(2)}, u32[]{:S(2)}) collective-permute-start(bf16[288,256]{1,0:T(8,128)(2,1)S(1)} %get-tuple-element.33), channel_id=1, source_target_pairs={{0,6},{1,25},{2,4},{3,27},{4,0},{5,29},{6,2},{7,31},{8,14},{9,1},{... | collective-permute-start | bytes 442376 | tf_op jit(solution)/shard_map/ppermute | solution.py:38
  20.5 5.7 %copy-start = (bf16[384,256]{1,0:T(8,128)(2,1)S(1)}, bf16[384,256]{1,0:T(8,128)(2,1)}, u32[]{:S(2)}) copy-start(bf16[384,256]{1,0:T(8,128)(2,1)} %refs_1_.5) | copy-start | bytes 589828
  20.5 9.1 %collective-permute-start.8 = (bf16[864,256]{1,0:T(8,128)(2,1)S(1)}, bf16[864,256]{1,0:T(8,128)(2,1)S(1)}, u32[]{:S(2)}, u32[]{:S(2)}) collective-permute-start(bf16[864,256]{1,0:T(8,128)(2,1)S(1)} %constant_dynamic-slice_fusion), channel_id=1, source_target_pairs={{0,16},{1,3},{2,18},{3,1},{4,20},{5,7},{6,22},{7,5},{8,24},{9,11},... | collective-permute-start | bytes 1327112 | tf_op jit(solution)/shard_map/ppermute | solution.py:38
  23.4 2.8 %copy-start.1 = (s32[64]{0:T(128)S(1)}, s32[64]{0:T(128)}, u32[]{:S(2)}) copy-start(s32[64]{0:T(128)} %refs_0_.1) | copy-start | bytes 772
  23.4 10.3 %collective-permute-start.6 = (bf16[768,256]{1,0:T(8,128)(2,1)S(1)}, bf16[768,256]{1,0:T(8,128)(2,1)S(1)}, u32[]{:S(2)}, u32[]{:S(2)}) collective-permute-start(bf16[768,256]{1,0:T(8,128)(2,1)S(1)} %get-tuple-element.26), channel_id=1, source_target_pairs={{0,8},{1,5},{2,10},{3,7},{4,12},{5,3},{6,14},{7,1},{8,16},{9,13},{... | collective-permute-start | bytes 1179656 | tf_op jit(solution)/shard_map/ppermute | solution.py:38
  23.9 10.1 %collective-permute-start.7 = (bf16[768,256]{1,0:T(8,128)(2,1)S(1)}, bf16[768,256]{1,0:T(8,128)(2,1)S(1)}, u32[]{:S(2)}, u32[]{:S(2)}) collective-permute-start(bf16[768,256]{1,0:T(8,128)(2,1)S(1)} %get-tuple-element.25), channel_id=1, source_target_pairs={{0,24},{1,7},{2,26},{3,5},{4,28},{5,1},{6,30},{7,3},{8,0},{9,15},{... | collective-permute-start | bytes 1179656 | tf_op jit(solution)/shard_map/ppermute | solution.py:38
  34.3 4.4 %collective-permute-start.9 = (f32[136,768]{1,0:T(8,128)S(1)}, f32[136,768]{1,0:T(8,128)S(1)}, u32[]{:S(2)}, u32[]{:S(2)}) collective-permute-start(f32[136,768]{1,0:T(8,128)S(1)} %shard_map.49), channel_id=1, source_target_pairs={{0,1},{1,0},{2,3},{3,2},{4,5},{5,4},{6,7},{7,6},{8,9},{9,8},{10,11... | collective-permute-start | bytes 1253384 | tf_op jit(solution)/shard_map/ppermute | solution.py:38
